TPU v7x, 256 devices: a whole 4x4x8 slice. The times are simulated.
256 devices in a mesh: gx: 32 (over z, y), gy: 8 (over x, core).
Axes of the slice: x: 4, y: 4, z: 8, core: 2. Of those that a mesh axis runs over, the one named last changes fastest.
Arguments:
- flow_state: float32 [5, 256, 4, 1024], P(None, 'gx', None, 'gy'), may hold values from -1 to 4, as said below
Outputs:
- increment: float32 [5, 256, 4, 1024], P(None, 'gx', None, 'gy')
Inputs may be any that keep to these rules, and one draw needn't show every extreme that they name: `flow_state`: density (component 0) lies between 0.6 and 1.4 and the pressure 0.4 (E - |m|^2 / (2 rho)) between 0.5 and 0.95 at every cell.
All inputs are finite; a program needn't handle non-finite values.
Results may differ from a plain program's by a relative error of at most 0.0003.
Values sent between devices are 32-bit elements; how exact they have to be, the bound alone decides.
No kernel may reach another device: no remote copies, remote signals or barrier semaphores. Data moves between devices by JAX's collectives and lax.ppermute only.
A program may use at most 256 MiB of HBM per device.

v0:
```python
import jax
import jax.numpy as jnp
from jax import lax
from jax.experimental import pallas as pl
from jax.experimental.pallas import tpu as pltpu
from jax.sharding import PartitionSpec as P

SPEED = 20.0
DAMP = 0.05
SCALE = SPEED / 3.0
SHARE = 1.0 / 3.0


def roll_lanes(value, amount):
    return value if amount % 128 == 0 else pltpu.roll(value, amount % 128, 1)


def roll_rows(value, amount):
    return value if amount % 8 == 0 else pltpu.roll(value, amount % 8, 0)


def lane_index():
    return lax.broadcasted_iota(jnp.int32, (8, 128), 1)


def row_index():
    return lax.broadcasted_iota(jnp.int32, (8, 128), 0)


def swap_bit(tiles, bit, width):
    shape = tiles[0].shape
    low = (lax.broadcasted_iota(jnp.int32, shape, 1) & width) == 0
    swapped = list(tiles)
    for i in range(len(tiles)):
        if not i & bit:
            first, second = tiles[i], tiles[i | bit]
            swapped[i] = jnp.where(low, first, roll_lanes(second, width))
            swapped[i | bit] = jnp.where(low, roll_lanes(first, -width), second)
    return swapped


def primitive(flow):
    inverse = 1.0 / flow[0]
    velocity = [flow[1] * inverse, flow[2] * inverse, flow[3] * inverse]
    squared = velocity[0] * velocity[0] + velocity[1] * velocity[1] + velocity[2] * velocity[2]
    pressure = 0.4 * (flow[4] - 0.5 * flow[0] * squared)
    return inverse, velocity, squared, pressure


def flux_along(flow, velocity, pressure, direction):
    moving = velocity[direction]
    pieces = [
        flow[1 + direction],
        flow[1] * moving,
        flow[2] * moving,
        flow[3] * moving,
        (flow[4] + pressure) * moving,
    ]
    pieces[1 + direction] = pieces[1 + direction] + pressure
    return pieces


def edge_kernel(flow_ref, edge_ref):
    lane = lane_index()
    packed = jnp.zeros((8, 128), jnp.float32)
    for v in range(20):
        tile = flow_ref[8 * v : 8 * v + 8, :]
        tail = (lane == 126 - 2 * v) | (lane == 127 - 2 * v)
        head = (lane == 2 * v) | (lane == 2 * v + 1)
        packed = jnp.where(tail, roll_lanes(tile, -2 * v), packed)
        packed = jnp.where(head, roll_lanes(tile, 2 * v), packed)
    edge_ref[...] = packed


def pack_kernel(flow_ref, left_ref, right_ref, out_ref):
    lane = lane_index()
    row = row_index()
    depth = row & 3
    left = left_ref[...]
    right = right_ref[...]
    both = [[None] * 8 for _ in range(5)]
    for xh in range(4):
        flow, edge = [], []
        for c in range(5):
            v = c * 4 + xh
            tile = flow_ref[8 * v : 8 * v + 8, :]
            flow.append(tile)
            beyond = jnp.where(lane < 2, roll_lanes(right, -2 * v), tile)
            edge.append(jnp.where(lane >= 126, roll_lanes(left, 2 * v), beyond))
        _, velocity, _, pressure = primitive(flow)
        along_y = flux_along(flow, velocity, pressure, 1)
        along_z = flux_along(flow, velocity, pressure, 2)
        _, edge_velocity, _, edge_pressure = primitive(edge)
        edge_y = flux_along(edge, edge_velocity, edge_pressure, 1)
        for c in range(5):
            q, e = flow[c], edge[c]
            minus_1 = roll_lanes(jnp.where(lane == 127, e, q), 1)
            minus_2 = roll_lanes(jnp.where(lane >= 126, e, q), 2)
            plus_1 = roll_lanes(jnp.where(lane == 0, e, q), -1)
            plus_2 = roll_lanes(jnp.where(lane < 2, e, q), -2)
            y_minus = roll_lanes(jnp.where(lane == 127, edge_y[c], along_y[c]), 1)
            y_plus = roll_lanes(jnp.where(lane == 0, edge_y[c], along_y[c]), -1)
            z = along_z[c]
            z_plus = jnp.where(depth == 3, roll_rows(z, 3), roll_rows(z, -1))
            z_minus = jnp.where(depth == 0, roll_rows(z, -3), roll_rows(z, 1))
            fourth = (plus_2 + minus_2) - 4.0 * (plus_1 + minus_1) + 6.0 * q
            partial = -SPEED * ((y_plus - y_minus) + (z_plus - z_minus)) - DAMP * fourth
            both[c][2 * xh] = jnp.where(row < 4, q, roll_rows(partial, 4))
            both[c][2 * xh + 1] = jnp.where(row < 4, roll_rows(q, 4), partial)
    for c in range(5):
        tiles = [both[c][(i & 1) * 4 + (i >> 2) * 2 + ((i >> 1) & 1)] for i in range(8)]
        tiles = swap_bit(tiles, 4, 64)
        tiles = swap_bit(tiles, 2, 32)
        tiles = swap_bit(tiles, 1, 16)
        for g in range(8):
            out_ref[pl.ds(g * 16 + c, 4, stride=128), :] = tiles[g][0:4]
            out_ref[pl.ds(g * 16 + 5 + c, 4, stride=128), :] = tiles[g][4:8]


def blocks_before(value, stride):
    if stride >= 8:
        return roll_rows(value, stride // 8)
    turned = roll_lanes(value, 16 * stride)
    return jnp.where(lane_index() < 16 * stride, roll_rows(turned, 1), turned)


def blocks_after(value, stride):
    if stride >= 8:
        return roll_rows(value, -(stride // 8))
    turned = roll_lanes(value, -16 * stride)
    return jnp.where(lane_index() >= 128 - 16 * stride, roll_rows(turned, -1), turned)


def jacobian_entries(flow):
    inverse, velocity, squared, pressure = primitive(flow)
    u, v, w = velocity
    f = 0.2 * squared
    h = (flow[4] + pressure) * inverse
    return [
        [None, 1.0, None, None, None],
        [f - u * u, 1.6 * u, -0.4 * v, -0.4 * w, 0.4],
        [-u * v, v, u, None, None],
        [-u * w, w, None, u, None],
        [u * (f - h), h - 0.4 * u * u, -0.4 * u * v, -0.4 * u * w, 1.4 * u],
    ], velocity, pressure


def scaled_plus(table, factor, shift):
    result = []
    for i in range(5):
        entries = []
        for j in range(5):
            entry = table[i][j]
            entry = None if entry is None else factor * entry
            if i == j:
                entry = shift if entry is None else entry + shift
            entries.append(entry)
        result.append(entries)
    return result


def kept_where(mask, table):
    return [[None if e is None else jnp.where(mask, e, 0.0) for e in row] for row in table]


def multiply(former, latter):
    columns = len(latter[0])
    result = []
    for i in range(5):
        entries = []
        for j in range(columns):
            total = None
            for k in range(5):
                if former[i][k] is None or latter[k][j] is None:
                    continue
                term = former[i][k] * latter[k][j]
                total = term if total is None else total + term
            entries.append(total)
        result.append(entries)
    return result


def add_tables(first, second):
    return [
        [b if a is None else (a if b is None else a + b) for a, b in zip(x, y)]
        for x, y in zip(first, second)
    ]


def identity_minus(table):
    return [[(1.0 - table[i][j]) if i == j else -table[i][j] for j in range(5)] for i in range(5)]


def dense(table):
    return [[e if hasattr(e, "shape") else jnp.full((8, 128), e, jnp.float32) for e in row] for row in table]


def solve(matrix, source):
    rows = [list(matrix[i]) + list(source[i]) for i in range(5)]
    width = len(rows[0])
    for k in range(5):
        if k < 4:
            largest = jnp.abs(rows[k][k])
            for j in range(k + 1, 5):
                candidate = jnp.abs(rows[j][k])
                better = candidate > largest
                largest = jnp.maximum(candidate, largest)
                for m in range(k, width):
                    upper, lower = rows[k][m], rows[j][m]
                    rows[k][m] = jnp.where(better, lower, upper)
                    rows[j][m] = jnp.where(better, upper, lower)
        inverse = 1.0 / rows[k][k]
        for m in range(k + 1, width):
            rows[k][m] = rows[k][m] * inverse
        for i in range(k + 1, 5):
            factor = rows[i][k]
            for m in range(k + 1, width):
                rows[i][m] = rows[i][m] - factor * rows[k][m]
    for k in range(4, 0, -1):
        for i in range(k):
            factor = rows[i][k]
            for m in range(5, width):
                rows[i][m] = rows[i][m] - factor * rows[k][m]
    return [rows[i][5:] for i in range(5)]


def side_by_side(*tables):
    return [sum((list(t[i]) for t in tables), []) for i in range(5)]


def columns_of(table, begin, end):
    return [row[begin:end] for row in table]


def mapped(function, table):
    return [[function(e) for e in row] for row in table]


def line_kernel(received_ref, out_ref):
    lane = lane_index()
    row = row_index()
    first_block = (row == 0) & (lane < 16)
    last_block = (row == 7) & (lane >= 112)

    def load(position):
        tiles = [received_ref[pl.ds(v * 16 + position, 8, stride=64), :] for v in range(4)]
        tiles = swap_bit(tiles, 2, 64)
        return swap_bit(tiles, 1, 32)

    flow = [load(c) for c in range(5)]
    partial = [load(5 + c) for c in range(5)]
    cells = {t: [flow[c][t] for c in range(5)] for t in range(4)}
    cells[-2] = [blocks_before(e, 1) for e in cells[2]]
    cells[-1] = [blocks_before(e, 1) for e in cells[3]]
    cells[4] = [blocks_after(e, 1) for e in cells[0]]
    cells[5] = [blocks_after(e, 1) for e in cells[1]]
    from_before, from_after, along_x = {}, {}, {}
    for t in range(-2, 5):
        table, velocity, pressure = jacobian_entries(cells[t])
        from_before[t] = scaled_plus(table, SCALE, SHARE)
        from_after[t] = scaled_plus(table, -SCALE, SHARE)
        along_x[t] = flux_along(cells[t], velocity, pressure, 0)
    from_before[-1] = kept_where(jnp.logical_not(first_block), from_before[-1])
    from_after[4] = kept_where(jnp.logical_not(last_block), from_after[4])
    right = {}
    for t in range(4):
        right[t] = []
        for c in range(5):
            fourth = (
                (cells[t + 2][c] + cells[t - 2][c])
                - 4.0 * (cells[t + 1][c] + cells[t - 1][c])
                + 6.0 * cells[t][c]
            )
            total = partial[c][t] - SPEED * (along_x[t + 1][c] - along_x[t - 1][c]) - DAMP * fourth
            right[t].append([total * SHARE])
    right[-1] = mapped(lambda e: blocks_before(e, 1), right[3])

    def eliminated(t):
        matrix = identity_minus(
            add_tables(
                multiply(from_after[t + 1], from_before[t]),
                multiply(from_before[t - 1], from_after[t]),
            )
        )
        before = dense(multiply(from_before[t - 1], from_before[t - 2]))
        after = dense(multiply(from_after[t + 1], from_after[t + 2]))
        value = add_tables(
            right[t],
            add_tables(
                multiply(from_after[t + 1], right[t + 1]), multiply(from_before[t - 1], right[t - 1])
            ),
        )
        return matrix, before, after, value

    def split(solved):
        return columns_of(solved, 0, 5), columns_of(solved, 5, 10), columns_of(solved, 10, 11)

    matrix, before, after, value = eliminated(2)
    half_before, half_after, half_value = split(solve(matrix, side_by_side(before, after, value)))
    matrix, before, after, value = eliminated(0)
    prior = lambda table: mapped(lambda e: blocks_before(e, 1), table)
    coupling = add_tables(multiply(after, half_before), multiply(before, prior(half_after)))
    matrix = [[m - c for m, c in zip(x, y)] for x, y in zip(matrix, coupling)]
    value = add_tables(
        value, add_tables(multiply(after, half_value), multiply(before, prior(half_value)))
    )
    before = multiply(before, prior(half_before))
    after = multiply(after, half_after)
    before, after, value = split(solve(matrix, side_by_side(before, after, value)))
    stride = 1
    while stride < 64:
        earlier = lambda table: mapped(lambda e: blocks_before(e, stride), table)
        later = lambda table: mapped(lambda e: blocks_after(e, stride), table)
        matrix = identity_minus(
            add_tables(multiply(before, earlier(after)), multiply(after, later(before)))
        )
        value = add_tables(
            value, add_tables(multiply(before, earlier(value)), multiply(after, later(value)))
        )
        if stride < 32:
            new_before = multiply(before, earlier(before))
            new_after = multiply(after, later(after))
            before, after, value = split(solve(matrix, side_by_side(new_before, new_after, value)))
        else:
            value = solve(matrix, value)
        stride *= 2
    result = {0: value}
    result[4] = mapped(lambda e: jnp.where(last_block, 0.0, blocks_after(e, 1)), value)
    result[2] = add_tables(
        half_value, add_tables(multiply(half_before, result[0]), multiply(half_after, result[4]))
    )
    for t in (1, 3):
        result[t] = add_tables(
            right[t],
            add_tables(
                multiply(from_before[t - 1], result[t - 1]), multiply(from_after[t + 1], result[t + 1])
            ),
        )
    for c in range(5):
        tiles = [result[t][c][0] for t in range(4)]
        tiles = swap_bit(tiles, 2, 64)
        tiles = swap_bit(tiles, 1, 32)
        for v in range(4):
            out_ref[pl.ds(v * 8 + c, 8, stride=32), :] = tiles[v]


def unpack_kernel(returned_ref, out_ref):
    for c in range(5):
        tiles = [returned_ref[pl.ds(g * 8 + c, 4, stride=64), :] for g in range(8)]
        tiles = swap_bit(tiles, 4, 64)
        tiles = swap_bit(tiles, 2, 32)
        tiles = swap_bit(tiles, 1, 16)
        for i in range(8):
            x = (i & 1) * 4 + (i >> 2) * 2 + ((i >> 1) & 1)
            out_ref[c * 32 + x * 4 : c * 32 + x * 4 + 4, :] = tiles[i]


def call(kernel, rows, *operands):
    whole = pl.BlockSpec(memory_space=pltpu.VMEM)
    return pl.pallas_call(
        kernel,
        out_shape=jax.ShapeDtypeStruct((rows, 128), jnp.float32),
        in_specs=[whole] * len(operands),
        out_specs=whole,
        compiler_params=pltpu.CompilerParams(vmem_limit_bytes=32 * 1024 * 1024),
    )(*operands)


def per_device(flow_state):
    flow = flow_state.reshape(160, 128)
    count = lax.axis_size("gy")
    edge = call(edge_kernel, 8, flow)
    left = lax.ppermute(edge, "gy", [(i, (i + 1) % count) for i in range(count)])
    right = lax.ppermute(edge, "gy", [((i + 1) % count, i) for i in range(count)])
    packed = call(pack_kernel, 512, flow, left, right)
    received = lax.all_to_all(
        packed.reshape(32, 16, 128), "gx", split_axis=0, concat_axis=0, tiled=True
    ).reshape(512, 128)
    solved = call(line_kernel, 256, received)
    returned = lax.all_to_all(
        solved.reshape(32, 8, 128), "gx", split_axis=0, concat_axis=0, tiled=True
    ).reshape(256, 128)
    return call(unpack_kernel, 160, returned).reshape(flow_state.shape)


def solution(mesh):
    placed = (P(None, "gx", None, "gy"),)
    return jax.shard_map(
        per_device, mesh=mesh, in_specs=placed, out_specs=P(None, "gx", None, "gy"), check_vma=False
    )
```

profile of v0, /device:TPU:6, one launch (start us, length us, event | category | flops | bytes accessed | tf_op | source)
XLA Modules:
  0.0 48.2 jit_solution(9192938212118236365)
XLA Ops:
  0.0 0.0 copy-start
  0.0 0.9 %copy-done = f32[5,8,4,128]{3,2,1,0:T(4,128)S(1)} copy-done((f32[5,8,4,128]{3,2,1,0:T(4,128)S(1)}, f32[5,8,4,128]{3,2,1,0:T(4,128)}, u32[]{:S(2)}) %copy-start) | copy-done | bytes 81944
  0.9 0.1 shard_map.17
  1.0 0.3 collective-permute-start.1
  1.3 0.2 collective-permute-start
  1.5 1.1 %collective-permute-done.1.right_ref = f32[8,128]{1,0:T(8,128)S(1)} collective-permute-done((f32[8,128]{1,0:T(8,128)S(1)}, f32[8,128]{1,0:T(8,128)S(1)}, u32[]{:S(2)}, u32[]{:S(2)}) %collective-permute-start.1) | collective-permute-done | bytes 4128 | tf_op jit(solution)/shard_map/ppermute | solution.py:374
  2.6 1.7 %collective-permute-done.left_ref = f32[8,128]{1,0:T(8,128)S(1)} collective-permute-done((f32[8,128]{1,0:T(8,128)S(1)}, f32[8,128]{1,0:T(8,128)S(1)}, u32[]{:S(2)}, u32[]{:S(2)}) %collective-permute-start) | collective-permute-done | bytes 4128 | tf_op jit(solution)/shard_map/ppermute | solution.py:373
  4.3 0.6 %shard_map.18 = f32[512,128]{1,0:T(8,128)S(1)} custom-call(f32[160,128]{1,0:T(8,128)S(1)} %bitcast.11, f32[8,128]{1,0:T(8,128)S(1)} %collective-permute-done.left_ref, f32[8,128]{1,0:T(8,128)S(1)} %collective-permute-done.1.right_ref), custom_call_target="tpu_custom_call" | custom-call | tf_op jit(solution)/shard_map/pallas_call | solution.py:360
  4.9 25.1 %all_to_all.10 = f32[32,16,128]{2,1,0:T(8,128)S(1)} all-to-all(f32[32,16,128]{2,1,0:T(8,128)S(1)} %bitcast.6), channel_id=1, replica_groups=mesh['gx'=32,'gy'=8] {'gx'}, dimensions={0} | all-to-all | bytes 524288 | tf_op jit(solution)/shard_map/all_to_all | solution.py:376
  30.1 3.0 %shard_map.19 = f32[256,128]{1,0:T(8,128)S(1)} custom-call(f32[512,128]{1,0:T(8,128)S(1)} %bitcast.7), custom_call_target="tpu_custom_call" | custom-call | tf_op jit(solution)/shard_map/pallas_call | solution.py:360
  33.1 14.2 %all_to_all.11 = f32[32,8,128]{2,1,0:T(8,128)S(1)} all-to-all(f32[32,8,128]{2,1,0:T(8,128)S(1)} %bitcast.8), channel_id=1, replica_groups=mesh['gx'=32,'gy'=8] {'gx'}, dimensions={0} | all-to-all | bytes 262144 | tf_op jit(solution)/shard_map/all_to_all | solution.py:380
  47.3 0.9 %shard_map.20 = f32[160,128]{1,0:T(8,128)} custom-call(f32[256,128]{1,0:T(8,128)S(1)} %bitcast.9), custom_call_target="tpu_custom_call" | custom-call | tf_op jit(solution)/shard_map/pallas_call | solution.py:360
Async XLA Ops:
  0.0 0.9 %copy-start = (f32[5,8,4,128]{3,2,1,0:T(4,128)S(1)}, f32[5,8,4,128]{3,2,1,0:T(4,128)}, u32[]{:S(2)}) copy-start(f32[5,8,4,128]{3,2,1,0:T(4,128)} %param.1) | copy-start | bytes 245764
  1.0 1.6 %collective-permute-start.1 = (f32[8,128]{1,0:T(8,128)S(1)}, f32[8,128]{1,0:T(8,128)S(1)}, u32[]{:S(2)}, u32[]{:S(2)}) collective-permute-start(f32[8,128]{1,0:T(8,128)S(1)} %shard_map.17), channel_id=1, source_target_pairs={{1,0},{2,1},{3,2},{4,3},{5,4},{6,5},{7,6},{0,7},{9,8},{10,9},{11,1... | collective-permute-start | bytes 12296 | tf_op jit(solution)/shard_map/ppermute | solution.py:374
  1.3 3.0 %collective-permute-start = (f32[8,128]{1,0:T(8,128)S(1)}, f32[8,128]{1,0:T(8,128)S(1)}, u32[]{:S(2)}, u32[]{:S(2)}) collective-permute-start(f32[8,128]{1,0:T(8,128)S(1)} %shard_map.17), channel_id=1, source_target_pairs={{0,1},{1,2},{2,3},{3,4},{4,5},{5,6},{6,7},{7,0},{8,9},{9,10},{10,1... | collective-permute-start | bytes 12296 | tf_op jit(solution)/shard_map/ppermute | solution.py:373
where the time goes:
time: 48.4 us; the launch traced here: 48.2 us
  blocking collectives  39.4 us (81%)
  Pallas kernels  4.6 us (10%)
  waiting for transfers between devices  2.79 us (6%)
  local copies, waits for them, and re-layouts  0.89 us (2%)
  starting transfers between devices  0.52 us (1%)
    all_to_all x1, blocking collectives, per_device(): lax.all_to_all(packed.reshape(32, 16, 128), 'gx', split_axis=0, concat_ax...  25.1 us
    all_to_all x1, blocking collectives, per_device(): lax.all_to_all(solved.reshape(32, 8, 128), 'gx', split_axis=0, concat_axi...  14.2 us
    pallas_call x4, Pallas kernels, call(): pl.pallas_call(kernel, out_shape=jax.ShapeDtypeStruct((rows, 128), jnp.fl...  4.6 us
    ppermute x1, waiting for transfers between devices, per_device(): lax.ppermute(edge, 'gy', [(i, (i + 1) % count) for i in range(count)])  1.7 us
    ppermute x1, waiting for transfers between devices, per_device(): lax.ppermute(edge, 'gy', [((i + 1) % count, i) for i in range(count)])  1.09 us
  transfers between devices with their start and end apart: 2, of which 2 were waited for; matrix products, arithmetic and copies ran while one was open for 0% of the time, Pallas kernels for 0%

commit v1 on v0

--- a/solution.py
+++ b/solution.py
@@ -113,8 +113,8 @@
         tiles = swap_bit(tiles, 2, 32)
         tiles = swap_bit(tiles, 1, 16)
         for g in range(8):
-            out_ref[pl.ds(g * 16 + c, 4, stride=128), :] = tiles[g][0:4]
-            out_ref[pl.ds(g * 16 + 5 + c, 4, stride=128), :] = tiles[g][4:8]
+            out_ref[pl.ds(g * 10 + c, 4, stride=80), :] = tiles[g][0:4]
+            out_ref[pl.ds(g * 10 + 5 + c, 4, stride=80), :] = tiles[g][4:8]
 
 
 def blocks_before(value, stride):
@@ -243,7 +243,7 @@
     last_block = (row == 7) & (lane >= 112)
 
     def load(position):
-        tiles = [received_ref[pl.ds(v * 16 + position, 8, stride=64), :] for v in range(4)]
+        tiles = [received_ref[pl.ds(v * 10 + position, 8, stride=40), :] for v in range(4)]
         tiles = swap_bit(tiles, 2, 64)
         return swap_bit(tiles, 1, 32)
 
@@ -341,12 +341,12 @@
         tiles = swap_bit(tiles, 2, 64)
         tiles = swap_bit(tiles, 1, 32)
         for v in range(4):
-            out_ref[pl.ds(v * 8 + c, 8, stride=32), :] = tiles[v]
+            out_ref[pl.ds(v * 5 + c, 8, stride=20), :] = tiles[v]
 
 
 def unpack_kernel(returned_ref, out_ref):
     for c in range(5):
-        tiles = [returned_ref[pl.ds(g * 8 + c, 4, stride=64), :] for g in range(8)]
+        tiles = [returned_ref[pl.ds(g * 5 + c, 4, stride=40), :] for g in range(8)]
         tiles = swap_bit(tiles, 4, 64)
         tiles = swap_bit(tiles, 2, 32)
         tiles = swap_bit(tiles, 1, 16)
@@ -372,14 +372,14 @@
     edge = call(edge_kernel, 8, flow)
     left = lax.ppermute(edge, "gy", [(i, (i + 1) % count) for i in range(count)])
     right = lax.ppermute(edge, "gy", [((i + 1) % count, i) for i in range(count)])
-    packed = call(pack_kernel, 512, flow, left, right)
+    packed = call(pack_kernel, 320, flow, left, right)
     received = lax.all_to_all(
-        packed.reshape(32, 16, 128), "gx", split_axis=0, concat_axis=0, tiled=True
-    ).reshape(512, 128)
-    solved = call(line_kernel, 256, received)
+        packed.reshape(32, 1, 1280), "gx", split_axis=0, concat_axis=0, tiled=True
+    ).reshape(320, 128)
+    solved = call(line_kernel, 160, received)
     returned = lax.all_to_all(
-        solved.reshape(32, 8, 128), "gx", split_axis=0, concat_axis=0, tiled=True
-    ).reshape(256, 128)
+        solved.reshape(32, 1, 640), "gx", split_axis=0, concat_axis=0, tiled=True
+    ).reshape(160, 128)
     return call(unpack_kernel, 160, returned).reshape(flow_state.shape)
 
 

time: 48.4 us -> 46.5 us (0.961); the launches traced: 48.2 us -> 45.6 us
  blocking collectives: 39.4 us -> 36.8 us
    all_to_all x2, blocking collectives: 39.4 us -> 36.8 us  [the longest x1 23.4 us: per_device(): lax.all_to_all(packed.reshape(32, 1, 1280), 'gx', split_axis=0, concat_ax...]
where the time goes in v1:
time: 46.5 us; the launch traced here: 45.6 us
  blocking collectives  36.8 us (79%)
  Pallas kernels  4.5 us (10%)
  waiting for transfers between devices  2.79 us (6%)
  local copies, waits for them, and re-layouts  0.89 us (2%)
  starting transfers between devices  0.52 us (1%)
    all_to_all x1, blocking collectives, per_device(): lax.all_to_all(packed.reshape(32, 1, 1280), 'gx', split_axis=0, concat_ax...  23.4 us
    all_to_all x1, blocking collectives, per_device(): lax.all_to_all(solved.reshape(32, 1, 640), 'gx', split_axis=0, concat_axi...  13.4 us
    pallas_call x4, Pallas kernels, call(): pl.pallas_call(kernel, out_shape=jax.ShapeDtypeStruct((rows, 128), jnp.fl...  4.5 us
    ppermute x1, waiting for transfers between devices, per_device(): lax.ppermute(edge, 'gy', [(i, (i + 1) % count) for i in range(count)])  1.7 us
    ppermute x1, waiting for transfers between devices, per_device(): lax.ppermute(edge, 'gy', [((i + 1) % count, i) for i in range(count)])  1.09 us
  transfers between devices with their start and end apart: 2, of which 2 were waited for; matrix products, arithmetic and copies ran while one was open for 0% of the time, Pallas kernels for 0%

profile of v1, /device:TPU:6, one launch (start us, length us, event | category | flops | bytes accessed | tf_op | source)
XLA Modules:
  0.0 45.6 jit_solution(1145928375798182418)
XLA Ops:
  0.0 0.0 copy-start
  0.0 0.9 %copy-done = f32[5,8,4,128]{3,2,1,0:T(4,128)S(1)} copy-done((f32[5,8,4,128]{3,2,1,0:T(4,128)S(1)}, f32[5,8,4,128]{3,2,1,0:T(4,128)}, u32[]{:S(2)}) %copy-start) | copy-done | bytes 81944
  0.9 0.1 shard_map.17
  1.0 0.3 collective-permute-start.1
  1.3 0.2 collective-permute-start
  1.5 1.1 %collective-permute-done.1.right_ref = f32[8,128]{1,0:T(8,128)S(1)} collective-permute-done((f32[8,128]{1,0:T(8,128)S(1)}, f32[8,128]{1,0:T(8,128)S(1)}, u32[]{:S(2)}, u32[]{:S(2)}) %collective-permute-start.1) | collective-permute-done | bytes 4128 | tf_op jit(solution)/shard_map/ppermute | solution.py:374
  2.6 1.7 %collective-permute-done.left_ref = f32[8,128]{1,0:T(8,128)S(1)} collective-permute-done((f32[8,128]{1,0:T(8,128)S(1)}, f32[8,128]{1,0:T(8,128)S(1)}, u32[]{:S(2)}, u32[]{:S(2)}) %collective-permute-start) | collective-permute-done | bytes 4128 | tf_op jit(solution)/shard_map/ppermute | solution.py:373
  4.3 0.6 %shard_map.18 = f32[320,128]{1,0:T(8,128)S(1)} custom-call(f32[160,128]{1,0:T(8,128)S(1)} %bitcast.9, f32[8,128]{1,0:T(8,128)S(1)} %collective-permute-done.left_ref, f32[8,128]{1,0:T(8,128)S(1)} %collective-permute-done.1.right_ref), custom_call_target="tpu_custom_call" | custom-call | tf_op jit(solution)/shard_map/pallas_call | solution.py:360
  4.9 23.4 %all_to_all.10 = f32[32,1,1280]{2,1,0:T(1,128)S(1)} all-to-all(f32[32,1,1280]{2,1,0:T(1,128)S(1)} %bitcast.6), channel_id=1, replica_groups=mesh['gx'=32,'gy'=8] {'gx'}, dimensions={0} | all-to-all | bytes 327680 | tf_op jit(solution)/shard_map/all_to_all | solution.py:376
  28.3 2.9 %shard_map.19 = f32[160,128]{1,0:T(8,128)S(1)} custom-call(f32[320,128]{1,0:T(8,128)S(1)} %bitcast.7), custom_call_target="tpu_custom_call" | custom-call | tf_op jit(solution)/shard_map/pallas_call | solution.py:360
  31.2 13.4 %all_to_all.11 = f32[32,1,640]{2,1,0:T(1,128)S(1)} all-to-all(f32[32,1,640]{2,1,0:T(1,128)S(1)} %bitcast.11), channel_id=1, replica_groups=mesh['gx'=32,'gy'=8] {'gx'}, dimensions={0} | all-to-all | bytes 163840 | tf_op jit(solution)/shard_map/all_to_all | solution.py:380
  44.7 0.9 %shard_map.20 = f32[160,128]{1,0:T(8,128)} custom-call(f32[160,128]{1,0:T(8,128)S(1)} %bitcast.10), custom_call_target="tpu_custom_call" | custom-call | tf_op jit(solution)/shard_map/pallas_call | solution.py:360
Async XLA Ops:
  0.0 0.9 %copy-start = (f32[5,8,4,128]{3,2,1,0:T(4,128)S(1)}, f32[5,8,4,128]{3,2,1,0:T(4,128)}, u32[]{:S(2)}) copy-start(f32[5,8,4,128]{3,2,1,0:T(4,128)} %param.1) | copy-start | bytes 245764
  1.0 1.6 %collective-permute-start.1 = (f32[8,128]{1,0:T(8,128)S(1)}, f32[8,128]{1,0:T(8,128)S(1)}, u32[]{:S(2)}, u32[]{:S(2)}) collective-permute-start(f32[8,128]{1,0:T(8,128)S(1)} %shard_map.17), channel_id=1, source_target_pairs={{1,0},{2,1},{3,2},{4,3},{5,4},{6,5},{7,6},{0,7},{9,8},{10,9},{11,1... | collective-permute-start | bytes 12296 | tf_op jit(solution)/shard_map/ppermute | solution.py:374
  1.3 3.0 %collective-permute-start = (f32[8,128]{1,0:T(8,128)S(1)}, f32[8,128]{1,0:T(8,128)S(1)}, u32[]{:S(2)}, u32[]{:S(2)}) collective-permute-start(f32[8,128]{1,0:T(8,128)S(1)} %shard_map.17), channel_id=1, source_target_pairs={{0,1},{1,2},{2,3},{3,4},{4,5},{5,6},{6,7},{7,0},{8,9},{9,10},{10,1... | collective-permute-start | bytes 12296 | tf_op jit(solution)/shard_map/ppermute | solution.py:373

commit v2 on v1

--- a/solution.py
+++ b/solution.py
@@ -108,13 +108,39 @@
             both[c][2 * xh] = jnp.where(row < 4, q, roll_rows(partial, 4))
             both[c][2 * xh + 1] = jnp.where(row < 4, roll_rows(q, 4), partial)
     for c in range(5):
-        tiles = [both[c][(i & 1) * 4 + (i >> 2) * 2 + ((i >> 1) & 1)] for i in range(8)]
+        tiles = both[c]
         tiles = swap_bit(tiles, 4, 64)
         tiles = swap_bit(tiles, 2, 32)
         tiles = swap_bit(tiles, 1, 16)
         for g in range(8):
             out_ref[pl.ds(g * 10 + c, 4, stride=80), :] = tiles[g][0:4]
             out_ref[pl.ds(g * 10 + 5 + c, 4, stride=80), :] = tiles[g][4:8]
+
+
+def swapped_halves(value):
+    return roll_rows(value, 4)
+
+
+def in_top(top, bottom):
+    return jnp.where(row_index() < 4, top, bottom)
+
+
+def half_before(value, periodic=False):
+    turned = roll_lanes(value, 16)
+    carried = roll_rows(turned, 5)
+    if periodic:
+        carried = jnp.where(row_index() == 0, roll_rows(turned, 1), carried)
+    earlier = jnp.where(lane_index() < 16, carried, roll_rows(turned, 4))
+    return in_top(earlier, roll_rows(value, 4))
+
+
+def half_after(value, periodic=False):
+    turned = roll_lanes(value, -16)
+    carried = roll_rows(turned, 3)
+    if periodic:
+        carried = jnp.where(row_index() == 7, roll_rows(turned, 7), carried)
+    later = jnp.where(lane_index() >= 112, carried, roll_rows(turned, 4))
+    return in_top(roll_rows(value, 4), later)
 
 
 def blocks_before(value, stride):
@@ -236,32 +262,48 @@
     return [[function(e) for e in row] for row in table]
 
 
+def both_halves(table):
+    return mapped(lambda e: e + swapped_halves(e), table)
+
+
+def minus(first, second):
+    return [[a - b for a, b in zip(x, y)] for x, y in zip(first, second)]
+
+
 def line_kernel(received_ref, out_ref):
     lane = lane_index()
     row = row_index()
-    first_block = (row == 0) & (lane < 16)
-    last_block = (row == 7) & (lane >= 112)
+    first_half = (row == 0) & (lane < 16)
+    last_half = (row == 7) & (lane >= 112)
+    straight = (row >= 4) == (lane >= 64)
+
+    def exchanged(tile):
+        return jnp.where(straight, tile, roll_lanes(swapped_halves(tile), 64))
 
     def load(position):
-        tiles = [received_ref[pl.ds(v * 10 + position, 8, stride=40), :] for v in range(4)]
-        tiles = swap_bit(tiles, 2, 64)
-        return swap_bit(tiles, 1, 32)
+        tiles = []
+        for u in range(4):
+            halves = [
+                received_ref[pl.ds((u + 4 * j) * 10 + position, 4, stride=80), :] for j in range(2)
+            ]
+            tiles.append(exchanged(jnp.concatenate(halves, axis=0)))
+        return swap_bit(swap_bit(tiles, 2, 32), 1, 16)
 
     flow = [load(c) for c in range(5)]
     partial = [load(5 + c) for c in range(5)]
     cells = {t: [flow[c][t] for c in range(5)] for t in range(4)}
-    cells[-2] = [blocks_before(e, 1) for e in cells[2]]
-    cells[-1] = [blocks_before(e, 1) for e in cells[3]]
-    cells[4] = [blocks_after(e, 1) for e in cells[0]]
-    cells[5] = [blocks_after(e, 1) for e in cells[1]]
+    cells[-2] = [half_before(e, True) for e in cells[2]]
+    cells[-1] = [half_before(e, True) for e in cells[3]]
+    cells[4] = [half_after(e, True) for e in cells[0]]
+    cells[5] = [half_after(e, True) for e in cells[1]]
     from_before, from_after, along_x = {}, {}, {}
     for t in range(-2, 5):
         table, velocity, pressure = jacobian_entries(cells[t])
         from_before[t] = scaled_plus(table, SCALE, SHARE)
         from_after[t] = scaled_plus(table, -SCALE, SHARE)
         along_x[t] = flux_along(cells[t], velocity, pressure, 0)
-    from_before[-1] = kept_where(jnp.logical_not(first_block), from_before[-1])
-    from_after[4] = kept_where(jnp.logical_not(last_block), from_after[4])
+    from_before[-1] = kept_where(jnp.logical_not(first_half), from_before[-1])
+    from_after[4] = kept_where(jnp.logical_not(last_half), from_after[4])
     right = {}
     for t in range(4):
         right[t] = []
@@ -273,7 +315,7 @@
             )
             total = partial[c][t] - SPEED * (along_x[t + 1][c] - along_x[t - 1][c]) - DAMP * fourth
             right[t].append([total * SHARE])
-    right[-1] = mapped(lambda e: blocks_before(e, 1), right[3])
+    right[-1] = mapped(half_before, right[3])
 
     def eliminated(t):
         matrix = identity_minus(
@@ -292,42 +334,74 @@
         )
         return matrix, before, after, value
 
-    def split(solved):
-        return columns_of(solved, 0, 5), columns_of(solved, 5, 10), columns_of(solved, 10, 11)
-
     matrix, before, after, value = eliminated(2)
-    half_before, half_after, half_value = split(solve(matrix, side_by_side(before, after, value)))
+    solved = solve(matrix, side_by_side(before, after, value))
+    fine_before, fine_after, fine_value = (
+        columns_of(solved, 0, 5), columns_of(solved, 5, 10), columns_of(solved, 10, 11)
+    )
     matrix, before, after, value = eliminated(0)
-    prior = lambda table: mapped(lambda e: blocks_before(e, 1), table)
-    coupling = add_tables(multiply(after, half_before), multiply(before, prior(half_after)))
-    matrix = [[m - c for m, c in zip(x, y)] for x, y in zip(matrix, coupling)]
+    matrix = minus(
+        matrix,
+        add_tables(
+            multiply(after, fine_before), multiply(before, mapped(half_before, fine_after))
+        ),
+    )
     value = add_tables(
-        value, add_tables(multiply(after, half_value), multiply(before, prior(half_value)))
+        value,
+        add_tables(multiply(after, fine_value), multiply(before, mapped(half_before, fine_value))),
     )
-    before = multiply(before, prior(half_before))
-    after = multiply(after, half_after)
-    before, after, value = split(solve(matrix, side_by_side(before, after, value)))
+    before = multiply(before, mapped(half_before, fine_before))
+    after = multiply(after, fine_after)
+
+    def pick(table, function):
+        return mapped(lambda e: function(e, swapped_halves(e)), table)
+
+    packed = [[in_top(a, swapped_halves(b)) for a, b in zip(x, y)] for x, y in zip(before, after)]
+    second = [[in_top(swapped_halves(a), b) for a, b in zip(x, y)] for x, y in zip(before, after)]
+    second_matrix = pick(matrix, lambda e, swapped: in_top(swapped, e))
+    second_value = pick(value, lambda e, swapped: in_top(swapped, e))
+    matrix = pick(matrix, in_top)
+    value = pick(value, in_top)
+    solved = solve(second_matrix, side_by_side(second, second_value))
+    second, second_value = columns_of(solved, 0, 5), columns_of(solved, 5, 6)
+
+    def top_before(table):
+        return mapped(lambda e: in_top(blocks_before(e, 1), e), table)
+
+    matrix = minus(matrix, both_halves(multiply(packed, mapped(half_before, second))))
+    value = add_tables(value, both_halves(multiply(packed, top_before(second_value))))
+    packed = multiply(packed, top_before(second))
+    solved = solve(matrix, side_by_side(packed, value))
+    packed, value = columns_of(solved, 0, 5), columns_of(solved, 5, 6)
+
     stride = 1
-    while stride < 64:
+    while stride < 32:
         earlier = lambda table: mapped(lambda e: blocks_before(e, stride), table)
         later = lambda table: mapped(lambda e: blocks_after(e, stride), table)
-        matrix = identity_minus(
-            add_tables(multiply(before, earlier(after)), multiply(after, later(before)))
-        )
-        value = add_tables(
-            value, add_tables(multiply(before, earlier(value)), multiply(after, later(value)))
-        )
-        if stride < 32:
-            new_before = multiply(before, earlier(before))
-            new_after = multiply(after, later(after))
-            before, after, value = split(solve(matrix, side_by_side(new_before, new_after, value)))
+        towards = lambda x, y: [[in_top(a, b) for a, b in zip(p, q)] for p, q in zip(x, y)]
+        prior, following = earlier(packed), later(packed)
+        crossed = mapped(swapped_halves, towards(following, prior))
+        matrix = identity_minus(both_halves(multiply(packed, crossed)))
+        beside = towards(earlier(value), later(value))
+        value = add_tables(value, both_halves(multiply(packed, beside)))
+        if stride < 16:
+            packed = multiply(packed, towards(prior, following))
+            solved = solve(matrix, side_by_side(packed, value))
+            packed, value = columns_of(solved, 0, 5), columns_of(solved, 5, 6)
         else:
             value = solve(matrix, value)
         stride *= 2
-    result = {0: value}
-    result[4] = mapped(lambda e: jnp.where(last_block, 0.0, blocks_after(e, 1)), value)
+
+    last_block = ((row & 3) == 3) & (lane >= 112)
+    ahead = mapped(lambda e: jnp.where(last_block, 0.0, blocks_after(e, 1)), value)
+    around = [[in_top(a[0], b[0])] for a, b in zip(value, ahead)]
+    middle = add_tables(second_value, both_halves(multiply(second, around)))
+    result = {
+        0: [[in_top(a[0], b[0])] for a, b in zip(value, middle)],
+        4: [[in_top(a[0], b[0])] for a, b in zip(middle, ahead)],
+    }
     result[2] = add_tables(
-        half_value, add_tables(multiply(half_before, result[0]), multiply(half_after, result[4]))
+        fine_value, add_tables(multiply(fine_before, result[0]), multiply(fine_after, result[4]))
     )
     for t in (1, 3):
         result[t] = add_tables(
@@ -337,11 +411,11 @@
             ),
         )
     for c in range(5):
-        tiles = [result[t][c][0] for t in range(4)]
-        tiles = swap_bit(tiles, 2, 64)
-        tiles = swap_bit(tiles, 1, 32)
-        for v in range(4):
-            out_ref[pl.ds(v * 5 + c, 8, stride=20), :] = tiles[v]
+        tiles = swap_bit(swap_bit([result[t][c][0] for t in range(4)], 2, 32), 1, 16)
+        for u in range(4):
+            tile = exchanged(tiles[u])
+            for j in range(2):
+                out_ref[pl.ds((u + 4 * j) * 5 + c, 4, stride=40), :] = tile[4 * j : 4 * j + 4]
 
 
 def unpack_kernel(returned_ref, out_ref):
@@ -350,9 +424,8 @@
         tiles = swap_bit(tiles, 4, 64)
         tiles = swap_bit(tiles, 2, 32)
         tiles = swap_bit(tiles, 1, 16)
-        for i in range(8):
-            x = (i & 1) * 4 + (i >> 2) * 2 + ((i >> 1) & 1)
-            out_ref[c * 32 + x * 4 : c * 32 + x * 4 + 4, :] = tiles[i]
+        for x in range(8):
+            out_ref[c * 32 + x * 4 : c * 32 + x * 4 + 4, :] = tiles[x]
 
 
 def call(kernel, rows, *operands):

time: 46.5 us -> 46.1 us (level)
  no operation moved by 1% of the time
where the time goes in v2:
time: 46.1 us; the launch traced here: 45.2 us
  blocking collectives  36.8 us (80%)
  Pallas kernels  4.13 us (9%)
  waiting for transfers between devices  2.79 us (6%)
  local copies, waits for them, and re-layouts  0.89 us (2%)
  starting transfers between devices  0.52 us (1%)
    all_to_all x1, blocking collectives, per_device(): lax.all_to_all(packed.reshape(32, 1, 1280), 'gx', split_axis=0, concat_ax...  23.4 us
    all_to_all x1, blocking collectives, per_device(): lax.all_to_all(solved.reshape(32, 1, 640), 'gx', split_axis=0, concat_axi...  13.4 us
    pallas_call x4, Pallas kernels, call(): pl.pallas_call(kernel, out_shape=jax.ShapeDtypeStruct((rows, 128), jnp.fl...  4.13 us
    ppermute x1, waiting for transfers between devices, per_device(): lax.ppermute(edge, 'gy', [(i, (i + 1) % count) for i in range(count)])  1.7 us
    ppermute x1, waiting for transfers between devices, per_device(): lax.ppermute(edge, 'gy', [((i + 1) % count, i) for i in range(count)])  1.09 us
  transfers between devices with their start and end apart: 2, of which 2 were waited for; matrix products, arithmetic and copies ran while one was open for 0% of the time, Pallas kernels for 0%

profile of v2, /device:TPU:6, one launch (start us, length us, event | category | flops | bytes accessed | tf_op | source)
XLA Modules:
  0.0 45.2 jit_solution(1149155029571907127)
XLA Ops:
  0.0 0.0 copy-start
  0.0 0.9 %copy-done = f32[5,8,4,128]{3,2,1,0:T(4,128)S(1)} copy-done((f32[5,8,4,128]{3,2,1,0:T(4,128)S(1)}, f32[5,8,4,128]{3,2,1,0:T(4,128)}, u32[]{:S(2)}) %copy-start) | copy-done | bytes 81944
  0.9 0.1 shard_map.17
  1.0 0.3 collective-permute-start.1
  1.3 0.2 collective-permute-start
  1.5 1.1 %collective-permute-done.1.right_ref = f32[8,128]{1,0:T(8,128)S(1)} collective-permute-done((f32[8,128]{1,0:T(8,128)S(1)}, f32[8,128]{1,0:T(8,128)S(1)}, u32[]{:S(2)}, u32[]{:S(2)}) %collective-permute-start.1) | collective-permute-done | bytes 4128 | tf_op jit(solution)/shard_map/ppermute | solution.py:447
  2.6 1.7 %collective-permute-done.left_ref = f32[8,128]{1,0:T(8,128)S(1)} collective-permute-done((f32[8,128]{1,0:T(8,128)S(1)}, f32[8,128]{1,0:T(8,128)S(1)}, u32[]{:S(2)}, u32[]{:S(2)}) %collective-permute-start) | collective-permute-done | bytes 4128 | tf_op jit(solution)/shard_map/ppermute | solution.py:446
  4.3 0.6 %shard_map.18 = f32[320,128]{1,0:T(8,128)S(1)} custom-call(f32[160,128]{1,0:T(8,128)S(1)} %bitcast.9, f32[8,128]{1,0:T(8,128)S(1)} %collective-permute-done.left_ref, f32[8,128]{1,0:T(8,128)S(1)} %collective-permute-done.1.right_ref), custom_call_target="tpu_custom_call" | custom-call | tf_op jit(solution)/shard_map/pallas_call | solution.py:433
  4.9 23.4 %all_to_all.10 = f32[32,1,1280]{2,1,0:T(1,128)S(1)} all-to-all(f32[32,1,1280]{2,1,0:T(1,128)S(1)} %bitcast.6), channel_id=1, replica_groups=mesh['gx'=32,'gy'=8] {'gx'}, dimensions={0} | all-to-all | bytes 327680 | tf_op jit(solution)/shard_map/all_to_all | solution.py:449
  28.3 2.6 %shard_map.19 = f32[160,128]{1,0:T(8,128)S(1)} custom-call(f32[320,128]{1,0:T(8,128)S(1)} %bitcast.7), custom_call_target="tpu_custom_call" | custom-call | tf_op jit(solution)/shard_map/pallas_call | solution.py:433
  30.9 13.4 %all_to_all.11 = f32[32,1,640]{2,1,0:T(1,128)S(1)} all-to-all(f32[32,1,640]{2,1,0:T(1,128)S(1)} %bitcast.11), channel_id=1, replica_groups=mesh['gx'=32,'gy'=8] {'gx'}, dimensions={0} | all-to-all | bytes 163840 | tf_op jit(solution)/shard_map/all_to_all | solution.py:453
  44.3 0.9 %shard_map.20 = f32[160,128]{1,0:T(8,128)} custom-call(f32[160,128]{1,0:T(8,128)S(1)} %bitcast.10), custom_call_target="tpu_custom_call" | custom-call | tf_op jit(solution)/shard_map/pallas_call | solution.py:433
Async XLA Ops:
  0.0 0.9 %copy-start = (f32[5,8,4,128]{3,2,1,0:T(4,128)S(1)}, f32[5,8,4,128]{3,2,1,0:T(4,128)}, u32[]{:S(2)}) copy-start(f32[5,8,4,128]{3,2,1,0:T(4,128)} %param.1) | copy-start | bytes 245764
  1.0 1.6 %collective-permute-start.1 = (f32[8,128]{1,0:T(8,128)S(1)}, f32[8,128]{1,0:T(8,128)S(1)}, u32[]{:S(2)}, u32[]{:S(2)}) collective-permute-start(f32[8,128]{1,0:T(8,128)S(1)} %shard_map.17), channel_id=1, source_target_pairs={{1,0},{2,1},{3,2},{4,3},{5,4},{6,5},{7,6},{0,7},{9,8},{10,9},{11,1... | collective-permute-start | bytes 12296 | tf_op jit(solution)/shard_map/ppermute | solution.py:447
  1.3 3.0 %collective-permute-start = (f32[8,128]{1,0:T(8,128)S(1)}, f32[8,128]{1,0:T(8,128)S(1)}, u32[]{:S(2)}, u32[]{:S(2)}) collective-permute-start(f32[8,128]{1,0:T(8,128)S(1)} %shard_map.17), channel_id=1, source_target_pairs={{0,1},{1,2},{2,3},{3,4},{4,5},{5,6},{6,7},{7,0},{8,9},{9,10},{10,1... | collective-permute-start | bytes 12296 | tf_op jit(solution)/shard_map/ppermute | solution.py:446

commit v3 on v2

--- a/solution.py
+++ b/solution.py
@@ -62,59 +62,79 @@
 
 def edge_kernel(flow_ref, edge_ref):
     lane = lane_index()
-    packed = jnp.zeros((8, 128), jnp.float32)
-    for v in range(20):
-        tile = flow_ref[8 * v : 8 * v + 8, :]
-        tail = (lane == 126 - 2 * v) | (lane == 127 - 2 * v)
-        head = (lane == 2 * v) | (lane == 2 * v + 1)
-        packed = jnp.where(tail, roll_lanes(tile, -2 * v), packed)
-        packed = jnp.where(head, roll_lanes(tile, 2 * v), packed)
-    edge_ref[...] = packed
-
-
-def pack_kernel(flow_ref, left_ref, right_ref, out_ref):
+    top = row_index() < 4
+    for c in range(5):
+        packed = None
+        for xh in range(4):
+            v = c * 4 + xh
+            tile = flow_ref[8 * v : 8 * v + 8, :]
+            turned = roll_lanes(tile, 16)
+            for xl in range(2):
+                if xl == 0:
+                    chosen = jnp.where(top, turned, roll_rows(tile, 4))
+                else:
+                    chosen = jnp.where(top, roll_rows(turned, 4), tile)
+                x = 2 * xh + xl
+                chosen = roll_lanes(chosen, 16 * x)
+                packed = chosen if packed is None else jnp.where(lane >= 16 * x, chosen, packed)
+        edge_ref[8 * c : 8 * c + 8, :] = packed
+
+
+def pack_kernel(flow_ref, out_ref):
     lane = lane_index()
     row = row_index()
     depth = row & 3
-    left = left_ref[...]
-    right = right_ref[...]
     both = [[None] * 8 for _ in range(5)]
     for xh in range(4):
-        flow, edge = [], []
+        flow = []
         for c in range(5):
             v = c * 4 + xh
-            tile = flow_ref[8 * v : 8 * v + 8, :]
-            flow.append(tile)
-            beyond = jnp.where(lane < 2, roll_lanes(right, -2 * v), tile)
-            edge.append(jnp.where(lane >= 126, roll_lanes(left, 2 * v), beyond))
+            flow.append(flow_ref[8 * v : 8 * v + 8, :])
         _, velocity, _, pressure = primitive(flow)
         along_y = flux_along(flow, velocity, pressure, 1)
         along_z = flux_along(flow, velocity, pressure, 2)
-        _, edge_velocity, _, edge_pressure = primitive(edge)
-        edge_y = flux_along(edge, edge_velocity, edge_pressure, 1)
         for c in range(5):
-            q, e = flow[c], edge[c]
-            minus_1 = roll_lanes(jnp.where(lane == 127, e, q), 1)
-            minus_2 = roll_lanes(jnp.where(lane >= 126, e, q), 2)
-            plus_1 = roll_lanes(jnp.where(lane == 0, e, q), -1)
-            plus_2 = roll_lanes(jnp.where(lane < 2, e, q), -2)
-            y_minus = roll_lanes(jnp.where(lane == 127, edge_y[c], along_y[c]), 1)
-            y_plus = roll_lanes(jnp.where(lane == 0, edge_y[c], along_y[c]), -1)
-            z = along_z[c]
+            q, y, z = flow[c], along_y[c], along_z[c]
+            far = jnp.where(lane < 2, 0.0, -DAMP * q)
+            plus = roll_lanes(jnp.where(lane == 0, 0.0, -SPEED * y + 4.0 * DAMP * q), -1)
+            minus_1 = roll_lanes(jnp.where(lane == 127, 0.0, SPEED * y + 4.0 * DAMP * q), 1)
+            plus = plus + roll_lanes(far, -2)
+            minus_1 = minus_1 + roll_lanes(jnp.where(lane >= 126, 0.0, -DAMP * q), 2)
             z_plus = jnp.where(depth == 3, roll_rows(z, 3), roll_rows(z, -1))
             z_minus = jnp.where(depth == 0, roll_rows(z, -3), roll_rows(z, 1))
-            fourth = (plus_2 + minus_2) - 4.0 * (plus_1 + minus_1) + 6.0 * q
-            partial = -SPEED * ((y_plus - y_minus) + (z_plus - z_minus)) - DAMP * fourth
+            partial = (plus + minus_1) - SPEED * (z_plus - z_minus) - 6.0 * DAMP * q
             both[c][2 * xh] = jnp.where(row < 4, q, roll_rows(partial, 4))
             both[c][2 * xh + 1] = jnp.where(row < 4, roll_rows(q, 4), partial)
     for c in range(5):
-        tiles = both[c]
-        tiles = swap_bit(tiles, 4, 64)
-        tiles = swap_bit(tiles, 2, 32)
-        tiles = swap_bit(tiles, 1, 16)
+        tiles = swap_bit(swap_bit(swap_bit(both[c], 4, 64), 2, 32), 1, 16)
         for g in range(8):
             out_ref[pl.ds(g * 10 + c, 4, stride=80), :] = tiles[g][0:4]
             out_ref[pl.ds(g * 10 + 5 + c, 4, stride=80), :] = tiles[g][4:8]
+
+
+def border_kernel(packed_ref, left_ref, right_ref, out_ref):
+    place = lane_index() & 15
+    top = row_index() < 4
+    distance = jnp.where(top, 15 - place, place)
+    nearest = distance == 0
+    next_two = distance < 2
+    sign = jnp.where(top, SPEED, -SPEED)
+    flow = []
+    for c in range(5):
+        flow.append(jnp.where(top, left_ref[8 * c : 8 * c + 8, :], right_ref[8 * c : 8 * c + 8, :]))
+    _, velocity, _, pressure = primitive(flow)
+    along_y = flux_along(flow, velocity, pressure, 1)
+    for c in range(5):
+        first = jnp.where(nearest, sign * along_y[c] + 4.0 * DAMP * flow[c], 0.0)
+        second = jnp.where(next_two, -DAMP * flow[c], 0.0)
+        total = jnp.where(
+            top,
+            roll_lanes(first, -15) + roll_lanes(second, -14),
+            roll_lanes(first, 15) + roll_lanes(second, 14),
+        )
+        for j, g in ((0, 0), (1, 7)):
+            rows = pl.ds(g * 10 + 5 + c, 4, stride=80)
+            out_ref[rows, :] = packed_ref[rows, :] + total[4 * j : 4 * j + 4]
 
 
 def swapped_halves(value):
@@ -428,7 +448,7 @@
             out_ref[c * 32 + x * 4 : c * 32 + x * 4 + 4, :] = tiles[x]
 
 
-def call(kernel, rows, *operands):
+def call(kernel, rows, *operands, **options):
     whole = pl.BlockSpec(memory_space=pltpu.VMEM)
     return pl.pallas_call(
         kernel,
@@ -436,16 +456,19 @@
         in_specs=[whole] * len(operands),
         out_specs=whole,
         compiler_params=pltpu.CompilerParams(vmem_limit_bytes=32 * 1024 * 1024),
+        **options,
     )(*operands)
 
 
 def per_device(flow_state):
     flow = flow_state.reshape(160, 128)
     count = lax.axis_size("gy")
-    edge = call(edge_kernel, 8, flow)
+    edge = call(edge_kernel, 40, flow)
     left = lax.ppermute(edge, "gy", [(i, (i + 1) % count) for i in range(count)])
     right = lax.ppermute(edge, "gy", [((i + 1) % count, i) for i in range(count)])
-    packed = call(pack_kernel, 320, flow, left, right)
+    cost = pl.CostEstimate(flops=4000000, bytes_accessed=250000, transcendentals=0)
+    packed = call(pack_kernel, 320, flow, cost_estimate=cost)
+    packed = call(border_kernel, 320, packed, left, right, input_output_aliases={0: 0})
     received = lax.all_to_all(
         packed.reshape(32, 1, 1280), "gx", split_axis=0, concat_axis=0, tiled=True
     ).reshape(320, 128)

time: 46.1 us -> 45.9 us (level)
    pallas_call x4 -> x5, Pallas kernels: 4.13 us -> 4.13 us  [call(): pl.pallas_call(kernel, out_shape=jax.ShapeDtypeStruct((rows, 128), jnp.fl...]
  transfers between devices with their start and end apart: 2 -> 2, of which waited for: 2 -> 2; matrix products, arithmetic and copies ran while one was open for 0% -> 0% of each run, Pallas kernels for 0% -> 1%
where the time goes in v3:
time: 45.9 us; the launch traced here: 45 us
  blocking collectives  36.8 us (80%)
  Pallas kernels  4.13 us (9%)
  waiting for transfers between devices  2.55 us (6%)
  local copies, waits for them, and re-layouts  0.89 us (2%)
  starting transfers between devices  0.52 us (1%)
    all_to_all x1, blocking collectives, per_device(): lax.all_to_all(packed.reshape(32, 1, 1280), 'gx', split_axis=0, concat_ax...  23.4 us
    all_to_all x1, blocking collectives, per_device(): lax.all_to_all(solved.reshape(32, 1, 640), 'gx', split_axis=0, concat_axi...  13.4 us
    pallas_call x5, Pallas kernels, call(): pl.pallas_call(kernel, out_shape=jax.ShapeDtypeStruct((rows, 128), jnp.fl...  4.13 us
    ppermute x1, waiting for transfers between devices, per_device(): lax.ppermute(edge, 'gy', [(i, (i + 1) % count) for i in range(count)])  1.73 us
  transfers between devices with their start and end apart: 2, of which 2 were waited for; matrix products, arithmetic and copies ran while one was open for 0% of the time, Pallas kernels for 1%

profile of v3, /device:TPU:6, one launch (start us, length us, event | category | flops | bytes accessed | tf_op | source)
XLA Modules:
  0.0 45.0 jit_solution(17833034597074661801)
XLA Ops:
  0.0 0.0 copy-start
  0.0 0.9 %copy-done = f32[5,8,4,128]{3,2,1,0:T(4,128)S(1)} copy-done((f32[5,8,4,128]{3,2,1,0:T(4,128)S(1)}, f32[5,8,4,128]{3,2,1,0:T(4,128)}, u32[]{:S(2)}) %copy-start) | copy-done | bytes 81944
  0.9 0.2 shard_map.18
  1.1 0.3 collective-permute-start.1
  1.3 0.2 collective-permute-start
  1.6 0.4 shard_map.17.packed_ref
  2.0 0.8 %collective-permute-done.1.right_ref = f32[40,128]{1,0:T(8,128)S(1)} collective-permute-done((f32[40,128]{1,0:T(8,128)S(1)}, f32[40,128]{1,0:T(8,128)S(1)}, u32[]{:S(2)}, u32[]{:S(2)}) %collective-permute-start.1) | collective-permute-done | bytes 20512 | tf_op jit(solution)/shard_map/ppermute | solution.py:468
  2.8 1.7 %collective-permute-done.left_ref = f32[40,128]{1,0:T(8,128)S(1)} collective-permute-done((f32[40,128]{1,0:T(8,128)S(1)}, f32[40,128]{1,0:T(8,128)S(1)}, u32[]{:S(2)}, u32[]{:S(2)}) %collective-permute-start) | collective-permute-done | bytes 20512 | tf_op jit(solution)/shard_map/ppermute | solution.py:467
  4.6 0.1 shard_map.19
  4.7 23.4 %all_to_all.10 = f32[32,1,1280]{2,1,0:T(1,128)S(1)} all-to-all(f32[32,1,1280]{2,1,0:T(1,128)S(1)} %bitcast.6), channel_id=1, replica_groups=mesh['gx'=32,'gy'=8] {'gx'}, dimensions={0} | all-to-all | bytes 327680 | tf_op jit(solution)/shard_map/all_to_all | solution.py:472
  28.1 2.6 %shard_map.20 = f32[160,128]{1,0:T(8,128)S(1)} custom-call(f32[320,128]{1,0:T(8,128)S(1)} %bitcast.7), custom_call_target="tpu_custom_call" | custom-call | tf_op jit(solution)/shard_map/pallas_call | solution.py:453
  30.6 13.4 %all_to_all.11 = f32[32,1,640]{2,1,0:T(1,128)S(1)} all-to-all(f32[32,1,640]{2,1,0:T(1,128)S(1)} %bitcast.11), channel_id=1, replica_groups=mesh['gx'=32,'gy'=8] {'gx'}, dimensions={0} | all-to-all | bytes 163840 | tf_op jit(solution)/shard_map/all_to_all | solution.py:476
  44.1 0.9 %shard_map.21 = f32[160,128]{1,0:T(8,128)} custom-call(f32[160,128]{1,0:T(8,128)S(1)} %bitcast.8), custom_call_target="tpu_custom_call" | custom-call | tf_op jit(solution)/shard_map/pallas_call | solution.py:453
Async XLA Ops:
  0.0 0.9 %copy-start = (f32[5,8,4,128]{3,2,1,0:T(4,128)S(1)}, f32[5,8,4,128]{3,2,1,0:T(4,128)}, u32[]{:S(2)}) copy-start(f32[5,8,4,128]{3,2,1,0:T(4,128)} %param.1) | copy-start | bytes 245764
  1.1 1.8 %collective-permute-start.1 = (f32[40,128]{1,0:T(8,128)S(1)}, f32[40,128]{1,0:T(8,128)S(1)}, u32[]{:S(2)}, u32[]{:S(2)}) collective-permute-start(f32[40,128]{1,0:T(8,128)S(1)} %shard_map.18), channel_id=1, source_target_pairs={{1,0},{2,1},{3,2},{4,3},{5,4},{6,5},{7,6},{0,7},{9,8},{10,9},{11,1... | collective-permute-start | bytes 61448 | tf_op jit(solution)/shard_map/ppermute | solution.py:468
  1.3 3.2 %collective-permute-start = (f32[40,128]{1,0:T(8,128)S(1)}, f32[40,128]{1,0:T(8,128)S(1)}, u32[]{:S(2)}, u32[]{:S(2)}) collective-permute-start(f32[40,128]{1,0:T(8,128)S(1)} %shard_map.18), channel_id=1, source_target_pairs={{0,1},{1,2},{2,3},{3,4},{4,5},{5,6},{6,7},{7,0},{8,9},{9,10},{10,1... | collective-permute-start | bytes 61448 | tf_op jit(solution)/shard_map/ppermute | solution.py:467

commit v4 on v3

--- a/solution.py
+++ b/solution.py
@@ -112,7 +112,9 @@
             out_ref[pl.ds(g * 10 + 5 + c, 4, stride=80), :] = tiles[g][4:8]
 
 
-def border_kernel(packed_ref, left_ref, right_ref, out_ref):
+def border_kernel(packed_ref, odd_ref, even_ref, out_ref):
+    is_top = (row_index() < 4).astype(jnp.int32)
+    by_odd = is_top == lax.rem(lax.axis_index("gy"), 2)
     place = lane_index() & 15
     top = row_index() < 4
     distance = jnp.where(top, 15 - place, place)
@@ -121,7 +123,7 @@
     sign = jnp.where(top, SPEED, -SPEED)
     flow = []
     for c in range(5):
-        flow.append(jnp.where(top, left_ref[8 * c : 8 * c + 8, :], right_ref[8 * c : 8 * c + 8, :]))
+        flow.append(jnp.where(by_odd, odd_ref[8 * c : 8 * c + 8, :], even_ref[8 * c : 8 * c + 8, :]))
     _, velocity, _, pressure = primitive(flow)
     along_y = flux_along(flow, velocity, pressure, 1)
     for c in range(5):
@@ -464,11 +466,13 @@
     flow = flow_state.reshape(160, 128)
     count = lax.axis_size("gy")
     edge = call(edge_kernel, 40, flow)
-    left = lax.ppermute(edge, "gy", [(i, (i + 1) % count) for i in range(count)])
-    right = lax.ppermute(edge, "gy", [((i + 1) % count, i) for i in range(count)])
+    exchanges = []
+    for start in (0, 1):
+        pairs = [((start + i) % count, (start + i + 1) % count) for i in range(0, count, 2)]
+        exchanges.append(lax.ppermute(edge, "gy", pairs + [(b, a) for a, b in pairs]))
     cost = pl.CostEstimate(flops=4000000, bytes_accessed=250000, transcendentals=0)
     packed = call(pack_kernel, 320, flow, cost_estimate=cost)
-    packed = call(border_kernel, 320, packed, left, right, input_output_aliases={0: 0})
+    packed = call(border_kernel, 320, packed, *exchanges, input_output_aliases={0: 0})
     received = lax.all_to_all(
         packed.reshape(32, 1, 1280), "gx", split_axis=0, concat_axis=0, tiled=True
     ).reshape(320, 128)

time: 45.9 us -> 45.2 us (0.985); the launches traced: 45 us -> 45 us
  waiting for transfers between devices: 2.55 us -> 0.47 us
  starting transfers between devices: 0.52 us -> 2.42 us
    ppermute x2, waiting for transfers between devices: 2.55 us -> 0.47 us  [per_device(): lax.ppermute(edge, 'gy', pairs + [(b, a) for a, b in pairs])]
    ppermute x2, starting transfers between devices: 0.52 us -> 2.42 us  [per_device(): lax.ppermute(edge, 'gy', pairs + [(b, a) for a, b in pairs])]
  transfers between devices with their start and end apart: 2 -> 2, of which waited for: 2 -> 1; matrix products, arithmetic and copies ran while one was open for 0% -> 0% of each run, Pallas kernels for 1% -> 1%
where the time goes in v4:
time: 45.2 us; the launch traced here: 45 us
  blocking collectives  37.1 us (82%)
  Pallas kernels  4.13 us (9%)
  starting transfers between devices  2.42 us (5%)
  local copies, waits for them, and re-layouts  0.89 us (2%)
  waiting for transfers between devices  0.47 us (1%)
    all_to_all x1, blocking collectives, per_device(): lax.all_to_all(packed.reshape(32, 1, 1280), 'gx', split_axis=0, concat_ax...  23.2 us
    all_to_all x1, blocking collectives, per_device(): lax.all_to_all(solved.reshape(32, 1, 640), 'gx', split_axis=0, concat_axi...  13.8 us
    pallas_call x5, Pallas kernels, call(): pl.pallas_call(kernel, out_shape=jax.ShapeDtypeStruct((rows, 128), jnp.fl...  4.13 us
    ppermute x2, starting transfers between devices, per_device(): lax.ppermute(edge, 'gy', pairs + [(b, a) for a, b in pairs])  2.42 us
  transfers between devices with their start and end apart: 2, of which 1 were waited for; matrix products, arithmetic and copies ran while one was open for 0% of the time, Pallas kernels for 1%

profile of v4, /device:TPU:6, one launch (start us, length us, event | category | flops | bytes accessed | tf_op | source)
XLA Modules:
  0.0 45.0 jit_solution(1077573349558422497)
XLA Ops:
  0.0 0.0 copy-start
  0.0 0.9 %copy-done = f32[5,8,4,128]{3,2,1,0:T(4,128)S(1)} copy-done((f32[5,8,4,128]{3,2,1,0:T(4,128)S(1)}, f32[5,8,4,128]{3,2,1,0:T(4,128)}, u32[]{:S(2)}) %copy-start) | copy-done | bytes 81944
  0.9 0.2 shard_map.18
  1.1 0.4 collective-permute-start.1
  1.4 2.1 %collective-permute-start = (f32[40,128]{1,0:T(8,128)S(1)}, f32[40,128]{1,0:T(8,128)S(1)}, u32[]{:S(2)}, u32[]{:S(2)}) collective-permute-start(f32[40,128]{1,0:T(8,128)S(1)} %shard_map.18), channel_id=1, source_target_pairs={{0,1},{2,3},{4,5},{6,7},{1,0},{3,2},{5,4},{7,6},{8,9},{10,11},{12,... | collective-permute-start | bytes 61448 | tf_op jit(solution)/shard_map/ppermute | solution.py:472
  3.5 0.4 shard_map.17.packed_ref
  3.9 0.5 %collective-permute-done.1.even_ref = f32[40,128]{1,0:T(8,128)S(1)} collective-permute-done((f32[40,128]{1,0:T(8,128)S(1)}, f32[40,128]{1,0:T(8,128)S(1)}, u32[]{:S(2)}, u32[]{:S(2)}) %collective-permute-start.1) | collective-permute-done | bytes 20512 | tf_op jit(solution)/shard_map/ppermute | solution.py:472
  4.4 0.0 collective-permute-done.odd_ref
  4.4 0.1 shard_map.19
  4.5 23.2 %all_to_all.10 = f32[32,1,1280]{2,1,0:T(1,128)S(1)} all-to-all(f32[32,1,1280]{2,1,0:T(1,128)S(1)} %bitcast.6), channel_id=1, replica_groups=mesh['gx'=32,'gy'=8] {'gx'}, dimensions={0} | all-to-all | bytes 327680 | tf_op jit(solution)/shard_map/all_to_all | solution.py:476
  27.7 2.6 %shard_map.20 = f32[160,128]{1,0:T(8,128)S(1)} custom-call(f32[320,128]{1,0:T(8,128)S(1)} %bitcast.7), custom_call_target="tpu_custom_call" | custom-call | tf_op jit(solution)/shard_map/pallas_call | solution.py:455
  30.3 13.8 %all_to_all.11 = f32[32,1,640]{2,1,0:T(1,128)S(1)} all-to-all(f32[32,1,640]{2,1,0:T(1,128)S(1)} %bitcast.11), channel_id=1, replica_groups=mesh['gx'=32,'gy'=8] {'gx'}, dimensions={0} | all-to-all | bytes 163840 | tf_op jit(solution)/shard_map/all_to_all | solution.py:480
  44.1 0.9 %shard_map.21 = f32[160,128]{1,0:T(8,128)} custom-call(f32[160,128]{1,0:T(8,128)S(1)} %bitcast.8), custom_call_target="tpu_custom_call" | custom-call | tf_op jit(solution)/shard_map/pallas_call | solution.py:455
Async XLA Ops:
  0.0 0.9 %copy-start = (f32[5,8,4,128]{3,2,1,0:T(4,128)S(1)}, f32[5,8,4,128]{3,2,1,0:T(4,128)}, u32[]{:S(2)}) copy-start(f32[5,8,4,128]{3,2,1,0:T(4,128)} %param.1) | copy-start | bytes 245764
  1.1 3.3 %collective-permute-start.1 = (f32[40,128]{1,0:T(8,128)S(1)}, f32[40,128]{1,0:T(8,128)S(1)}, u32[]{:S(2)}, u32[]{:S(2)}) collective-permute-start(f32[40,128]{1,0:T(8,128)S(1)} %shard_map.18), channel_id=1, source_target_pairs={{1,2},{3,4},{5,6},{7,0},{2,1},{4,3},{6,5},{0,7},{9,10},{11,12},{13... | collective-permute-start | bytes 61448 | tf_op jit(solution)/shard_map/ppermute | solution.py:472
  1.4 2.9 %collective-permute-start = (f32[40,128]{1,0:T(8,128)S(1)}, f32[40,128]{1,0:T(8,128)S(1)}, u32[]{:S(2)}, u32[]{:S(2)}) collective-permute-start(f32[40,128]{1,0:T(8,128)S(1)} %shard_map.18), channel_id=1, source_target_pairs={{0,1},{2,3},{4,5},{6,7},{1,0},{3,2},{5,4},{7,6},{8,9},{10,11},{12,... | collective-permute-start | bytes 61448 | tf_op jit(solution)/shard_map/ppermute | solution.py:472

commit v5 on v4

--- a/solution.py
+++ b/solution.py
@@ -60,14 +60,15 @@
     return pieces
 
 
-def edge_kernel(flow_ref, edge_ref):
+def edge_kernel(*refs):
+    flow_refs, (odd_ref, even_ref) = refs[:5], refs[5:]
+    swapped_by = jnp.zeros((8, 128), jnp.int32) + lax.rem(lax.axis_index("gy"), 2) == 1
     lane = lane_index()
     top = row_index() < 4
     for c in range(5):
         packed = None
         for xh in range(4):
-            v = c * 4 + xh
-            tile = flow_ref[8 * v : 8 * v + 8, :]
+            tile = flow_refs[c][8 * xh : 8 * xh + 8, :]
             turned = roll_lanes(tile, 16)
             for xl in range(2):
                 if xl == 0:
@@ -77,10 +78,13 @@
                 x = 2 * xh + xl
                 chosen = roll_lanes(chosen, 16 * x)
                 packed = chosen if packed is None else jnp.where(lane >= 16 * x, chosen, packed)
-        edge_ref[8 * c : 8 * c + 8, :] = packed
-
-
-def pack_kernel(flow_ref, out_ref):
+        turned = jnp.where(swapped_by, roll_rows(packed, 4), packed)
+        odd_ref[4 * c : 4 * c + 4, :] = turned[0:4]
+        even_ref[4 * c : 4 * c + 4, :] = turned[4:8]
+
+
+def pack_kernel(*refs):
+    flow_refs, out_ref = refs[:5], refs[5]
     lane = lane_index()
     row = row_index()
     depth = row & 3
@@ -88,8 +92,7 @@
     for xh in range(4):
         flow = []
         for c in range(5):
-            v = c * 4 + xh
-            flow.append(flow_ref[8 * v : 8 * v + 8, :])
+            flow.append(flow_refs[c][8 * xh : 8 * xh + 8, :])
         _, velocity, _, pressure = primitive(flow)
         along_y = flux_along(flow, velocity, pressure, 1)
         along_z = flux_along(flow, velocity, pressure, 2)
@@ -113,8 +116,7 @@
 
 
 def border_kernel(packed_ref, odd_ref, even_ref, out_ref):
-    is_top = (row_index() < 4).astype(jnp.int32)
-    by_odd = is_top == lax.rem(lax.axis_index("gy"), 2)
+    by_odd = jnp.zeros((8, 128), jnp.int32) + lax.rem(lax.axis_index("gy"), 2) == 1
     place = lane_index() & 15
     top = row_index() < 4
     distance = jnp.where(top, 15 - place, place)
@@ -123,7 +125,9 @@
     sign = jnp.where(top, SPEED, -SPEED)
     flow = []
     for c in range(5):
-        flow.append(jnp.where(by_odd, odd_ref[8 * c : 8 * c + 8, :], even_ref[8 * c : 8 * c + 8, :]))
+        beyond = [ref[4 * c : 4 * c + 4, :] for ref in (even_ref, odd_ref)]
+        beyond = jnp.concatenate(beyond, axis=0)
+        flow.append(jnp.where(by_odd, roll_rows(beyond, 4), beyond))
     _, velocity, _, pressure = primitive(flow)
     along_y = flux_along(flow, velocity, pressure, 1)
     for c in range(5):
@@ -463,15 +467,22 @@
 
 
 def per_device(flow_state):
-    flow = flow_state.reshape(160, 128)
+    flow = [flow_state[c].reshape(32, 128) for c in range(5)]
     count = lax.axis_size("gy")
-    edge = call(edge_kernel, 40, flow)
-    exchanges = []
-    for start in (0, 1):
+    vmem = pl.BlockSpec(memory_space=pltpu.VMEM)
+    edges = pl.pallas_call(
+        edge_kernel,
+        out_shape=[jax.ShapeDtypeStruct((20, 128), jnp.float32)] * 2,
+        in_specs=[vmem] * 5,
+        out_specs=[vmem] * 2,
+        compiler_params=pltpu.CompilerParams(vmem_limit_bytes=32 * 1024 * 1024),
+    )(*flow)
+    exchanges = [None, None]
+    for start in (1, 0):
         pairs = [((start + i) % count, (start + i + 1) % count) for i in range(0, count, 2)]
-        exchanges.append(lax.ppermute(edge, "gy", pairs + [(b, a) for a, b in pairs]))
+        exchanges[start] = lax.ppermute(edges[start], "gy", pairs + [(b, a) for a, b in pairs])
     cost = pl.CostEstimate(flops=4000000, bytes_accessed=250000, transcendentals=0)
-    packed = call(pack_kernel, 320, flow, cost_estimate=cost)
+    packed = call(pack_kernel, 320, *flow, cost_estimate=cost)
     packed = call(border_kernel, 320, packed, *exchanges, input_output_aliases={0: 0})
     received = lax.all_to_all(
         packed.reshape(32, 1, 1280), "gx", split_axis=0, concat_axis=0, tiled=True

time: 45.2 us -> 44.9 us (level)
  starting transfers between devices: 2.42 us -> 1.02 us
  waiting for transfers between devices: 0.47 us -> 1.85 us
    ppermute x2, starting transfers between devices: 2.42 us -> 1.02 us  [per_device(): lax.ppermute(edges[start], 'gy', pairs + [(b, a) for a, b in pairs])]
    ppermute x2, waiting for transfers between devices: 0.47 us -> 1.85 us  [per_device(): lax.ppermute(edges[start], 'gy', pairs + [(b, a) for a, b in pairs])]
    unnamed x2 -> x0, local copies, waits for them, and re-layouts: 0.89 us -> none
    slice x0 -> x1, local copies, waits for them, and re-layouts: none -> 0.79 us  [per_device(): flow = [flow_state[c].reshape(32, 128) for c in range(5)]]
    pallas_call x5 -> x4, Pallas kernels: 4.13 us -> 3.96 us  [call(): pl.pallas_call(kernel, out_shape=jax.ShapeDtypeStruct((rows, 128), jnp.fl...]
where the time goes in v5:
time: 44.9 us; the launch traced here: 44.6 us
  blocking collectives  36.7 us (82%)
  Pallas kernels  4.14 us (9%)
  waiting for transfers between devices  1.85 us (4%)
  starting transfers between devices  1.02 us (2%)
  local copies, waits for them, and re-layouts  0.79 us (2%)
    all_to_all x1, blocking collectives, per_device(): lax.all_to_all(packed.reshape(32, 1, 1280), 'gx', split_axis=0, concat_ax...  23 us
    all_to_all x1, blocking collectives, per_device(): lax.all_to_all(solved.reshape(32, 1, 640), 'gx', split_axis=0, concat_axi...  13.7 us
    pallas_call x4, Pallas kernels, call(): pl.pallas_call(kernel, out_shape=jax.ShapeDtypeStruct((rows, 128), jnp.fl...  3.96 us
    ppermute x2, waiting for transfers between devices, per_device(): lax.ppermute(edges[start], 'gy', pairs + [(b, a) for a, b in pairs])  1.85 us
    ppermute x2, starting transfers between devices, per_device(): lax.ppermute(edges[start], 'gy', pairs + [(b, a) for a, b in pairs])  1.02 us
  transfers between devices with their start and end apart: 2, of which 1 were waited for; matrix products, arithmetic and copies ran while one was open for 0% of the time, Pallas kernels for 1%

profile of v5, /device:TPU:6, one launch (start us, length us, event | category | flops | bytes accessed | tf_op | source)
XLA Modules:
  0.0 44.6 jit_solution(13030855168403666750)
XLA Ops:
  0.0 0.8 %fusion = (f32[1,8,4,128]{3,2,1,0:T(4,128)S(1)}, f32[1,8,4,128]{3,2,1,0:T(4,128)S(1)}, f32[1,8,4,128]{3,2,1,0:T(4,128)S(1)}, f32[1,8,4,128]{3,2,1,0:T(4,128)S(1)}, f32[1,8,4,128]{3,2,1,0:T(4,128)S(1)}) fusion(f32[5,8,4,128]{3,2,1,0:T(4,128)} %param.1), kind=kLoop, calls=%fused_computation | loop fusion | bytes 163840 | tf_op jit(solution)/shard_map/slice | solution.py:470
  0.8 0.2 shard_map.18
  1.0 0.1 collective-permute-start
  1.1 0.9 %collective-permute-start.1 = (f32[20,128]{1,0:T(8,128)S(1)}, f32[20,128]{1,0:T(8,128)S(1)}, u32[]{:S(2)}, u32[]{:S(2)}) collective-permute-start(f32[20,128]{1,0:T(8,128)S(1)} %get-tuple-element.8), channel_id=1, source_target_pairs={{1,2},{3,4},{5,6},{7,0},{2,1},{4,3},{6,5},{0,7},{9,10},{11,12},{13... | collective-permute-start | bytes 30728 | tf_op jit(solution)/shard_map/ppermute | solution.py:483
  2.0 0.4 shard_map.17.packed_ref
  2.4 0.0 collective-permute-done.odd_ref
  2.4 1.9 %collective-permute-done.1.even_ref = f32[20,128]{1,0:T(8,128)S(1)} collective-permute-done((f32[20,128]{1,0:T(8,128)S(1)}, f32[20,128]{1,0:T(8,128)S(1)}, u32[]{:S(2)}, u32[]{:S(2)}) %collective-permute-start.1) | collective-permute-done | bytes 10272 | tf_op jit(solution)/shard_map/ppermute | solution.py:483
  4.3 0.1 shard_map.19
  4.4 23.0 %all_to_all.10 = f32[32,1,1280]{2,1,0:T(1,128)S(1)} all-to-all(f32[32,1,1280]{2,1,0:T(1,128)S(1)} %bitcast.10), channel_id=1, replica_groups=mesh['gx'=32,'gy'=8] {'gx'}, dimensions={0} | all-to-all | bytes 327680 | tf_op jit(solution)/shard_map/all_to_all | solution.py:487
  27.4 2.6 %shard_map.20 = f32[160,128]{1,0:T(8,128)S(1)} custom-call(f32[320,128]{1,0:T(8,128)S(1)} %bitcast.11), custom_call_target="tpu_custom_call" | custom-call | tf_op jit(solution)/shard_map/pallas_call | solution.py:459
  30.0 13.7 %all_to_all.11 = f32[32,1,640]{2,1,0:T(1,128)S(1)} all-to-all(f32[32,1,640]{2,1,0:T(1,128)S(1)} %bitcast.13), channel_id=1, replica_groups=mesh['gx'=32,'gy'=8] {'gx'}, dimensions={0} | all-to-all | bytes 163840 | tf_op jit(solution)/shard_map/all_to_all | solution.py:491
  43.7 0.9 %shard_map.21 = f32[160,128]{1,0:T(8,128)} custom-call(f32[160,128]{1,0:T(8,128)S(1)} %bitcast.12), custom_call_target="tpu_custom_call" | custom-call | tf_op jit(solution)/shard_map/pallas_call | solution.py:459
Async XLA Ops:
  1.0 1.4 %collective-permute-start = (f32[20,128]{1,0:T(8,128)S(1)}, f32[20,128]{1,0:T(8,128)S(1)}, u32[]{:S(2)}, u32[]{:S(2)}) collective-permute-start(f32[20,128]{1,0:T(8,128)S(1)} %get-tuple-element.7), channel_id=1, source_target_pairs={{0,1},{2,3},{4,5},{6,7},{1,0},{3,2},{5,4},{7,6},{8,9},{10,11},{12,... | collective-permute-start | bytes 30728 | tf_op jit(solution)/shard_map/ppermute | solution.py:483
  1.1 3.2 %collective-permute-start.1 = (f32[20,128]{1,0:T(8,128)S(1)}, f32[20,128]{1,0:T(8,128)S(1)}, u32[]{:S(2)}, u32[]{:S(2)}) collective-permute-start(f32[20,128]{1,0:T(8,128)S(1)} %get-tuple-element.8), channel_id=1, source_target_pairs={{1,2},{3,4},{5,6},{7,0},{2,1},{4,3},{6,5},{0,7},{9,10},{11,12},{13... | collective-permute-start | bytes 30728 | tf_op jit(solution)/shard_map/ppermute | solution.py:483

commit v6 on v5

--- a/solution.py
+++ b/solution.py
@@ -61,7 +61,7 @@
 
 
 def edge_kernel(*refs):
-    flow_refs, (odd_ref, even_ref) = refs[:5], refs[5:]
+    flow_refs, (even_ref, odd_ref) = refs[:5], refs[5:]
     swapped_by = jnp.zeros((8, 128), jnp.int32) + lax.rem(lax.axis_index("gy"), 2) == 1
     lane = lane_index()
     top = row_index() < 4
@@ -115,7 +115,7 @@
             out_ref[pl.ds(g * 10 + 5 + c, 4, stride=80), :] = tiles[g][4:8]
 
 
-def border_kernel(packed_ref, odd_ref, even_ref, out_ref):
+def border_kernel(packed_ref, even_ref, odd_ref, out_ref):
     by_odd = jnp.zeros((8, 128), jnp.int32) + lax.rem(lax.axis_index("gy"), 2) == 1
     place = lane_index() & 15
     top = row_index() < 4
@@ -478,12 +478,12 @@
         compiler_params=pltpu.CompilerParams(vmem_limit_bytes=32 * 1024 * 1024),
     )(*flow)
     exchanges = [None, None]
-    for start in (1, 0):
+    for start in (0, 1):
         pairs = [((start + i) % count, (start + i + 1) % count) for i in range(0, count, 2)]
-        exchanges[start] = lax.ppermute(edges[start], "gy", pairs + [(b, a) for a, b in pairs])
+        exchanges[start] = lax.ppermute(edges[1 - start], "gy", pairs + [(b, a) for a, b in pairs])
     cost = pl.CostEstimate(flops=4000000, bytes_accessed=250000, transcendentals=0)
     packed = call(pack_kernel, 320, *flow, cost_estimate=cost)
-    packed = call(border_kernel, 320, packed, *exchanges, input_output_aliases={0: 0})
+    packed = call(border_kernel, 320, packed, *exchanges[::-1], input_output_aliases={0: 0})
     received = lax.all_to_all(
         packed.reshape(32, 1, 1280), "gx", split_axis=0, concat_axis=0, tiled=True
     ).reshape(320, 128)

time: 44.9 us -> 45.1 us (level)
  waiting for transfers between devices: 1.85 us -> 0.42 us
  starting transfers between devices: 1.02 us -> 2.42 us
    ppermute x2, waiting for transfers between devices: 1.85 us -> 0.42 us  [per_device(): lax.ppermute(edges[1 - start], 'gy', pairs + [(b, a) for a, b in pairs])]
    ppermute x2, starting transfers between devices: 1.02 us -> 2.42 us  [per_device(): lax.ppermute(edges[1 - start], 'gy', pairs + [(b, a) for a, b in pairs])]
where the time goes in v6:
time: 45.1 us; the launch traced here: 44.8 us
  blocking collectives  37 us (82%)
  Pallas kernels  4.14 us (9%)
  starting transfers between devices  2.42 us (5%)
  local copies, waits for them, and re-layouts  0.79 us (2%)
    all_to_all x1, blocking collectives, per_device(): lax.all_to_all(packed.reshape(32, 1, 1280), 'gx', split_axis=0, concat_ax...  23.2 us
    all_to_all x1, blocking collectives, per_device(): lax.all_to_all(solved.reshape(32, 1, 640), 'gx', split_axis=0, concat_axi...  13.8 us
    pallas_call x4, Pallas kernels, call(): pl.pallas_call(kernel, out_shape=jax.ShapeDtypeStruct((rows, 128), jnp.fl...  3.96 us
    ppermute x2, starting transfers between devices, per_device(): lax.ppermute(edges[1 - start], 'gy', pairs + [(b, a) for a, b in pairs])  2.42 us
  transfers between devices with their start and end apart: 2, of which 1 were waited for; matrix products, arithmetic and copies ran while one was open for 0% of the time, Pallas kernels for 1%

profile of v6, /device:TPU:6, one launch (start us, length us, event | category | flops | bytes accessed | tf_op | source)
XLA Modules:
  0.0 44.8 jit_solution(5454610218448860608)
XLA Ops:
  0.0 0.8 %fusion = (f32[1,8,4,128]{3,2,1,0:T(4,128)S(1)}, f32[1,8,4,128]{3,2,1,0:T(4,128)S(1)}, f32[1,8,4,128]{3,2,1,0:T(4,128)S(1)}, f32[1,8,4,128]{3,2,1,0:T(4,128)S(1)}, f32[1,8,4,128]{3,2,1,0:T(4,128)S(1)}) fusion(f32[5,8,4,128]{3,2,1,0:T(4,128)} %param.1), kind=kLoop, calls=%fused_computation | loop fusion | bytes 163840 | tf_op jit(solution)/shard_map/slice | solution.py:470
  0.8 0.2 shard_map.18
  1.0 0.4 collective-permute-start
  1.3 2.1 %collective-permute-start.1 = (f32[20,128]{1,0:T(8,128)S(1)}, f32[20,128]{1,0:T(8,128)S(1)}, u32[]{:S(2)}, u32[]{:S(2)}) collective-permute-start(f32[20,128]{1,0:T(8,128)S(1)} %get-tuple-element.8), channel_id=1, source_target_pairs={{0,1},{2,3},{4,5},{6,7},{1,0},{3,2},{5,4},{7,6},{8,9},{10,11},{12,... | collective-permute-start | bytes 30728 | tf_op jit(solution)/shard_map/ppermute | solution.py:483
  3.4 0.4 shard_map.17.packed_ref
  3.8 0.4 collective-permute-done.even_ref
  4.2 0.0 collective-permute-done.1.odd_ref
  4.2 0.1 shard_map.19
  4.3 23.2 %all_to_all.10 = f32[32,1,1280]{2,1,0:T(1,128)S(1)} all-to-all(f32[32,1,1280]{2,1,0:T(1,128)S(1)} %bitcast.10), channel_id=1, replica_groups=mesh['gx'=32,'gy'=8] {'gx'}, dimensions={0} | all-to-all | bytes 327680 | tf_op jit(solution)/shard_map/all_to_all | solution.py:487
  27.5 2.6 %shard_map.20 = f32[160,128]{1,0:T(8,128)S(1)} custom-call(f32[320,128]{1,0:T(8,128)S(1)} %bitcast.11), custom_call_target="tpu_custom_call" | custom-call | tf_op jit(solution)/shard_map/pallas_call | solution.py:459
  30.1 13.8 %all_to_all.11 = f32[32,1,640]{2,1,0:T(1,128)S(1)} all-to-all(f32[32,1,640]{2,1,0:T(1,128)S(1)} %bitcast.13), channel_id=1, replica_groups=mesh['gx'=32,'gy'=8] {'gx'}, dimensions={0} | all-to-all | bytes 163840 | tf_op jit(solution)/shard_map/all_to_all | solution.py:491
  43.9 0.9 %shard_map.21 = f32[160,128]{1,0:T(8,128)} custom-call(f32[160,128]{1,0:T(8,128)S(1)} %bitcast.12), custom_call_target="tpu_custom_call" | custom-call | tf_op jit(solution)/shard_map/pallas_call | solution.py:459
Async XLA Ops:
  1.0 3.2 %collective-permute-start = (f32[20,128]{1,0:T(8,128)S(1)}, f32[20,128]{1,0:T(8,128)S(1)}, u32[]{:S(2)}, u32[]{:S(2)}) collective-permute-start(f32[20,128]{1,0:T(8,128)S(1)} %get-tuple-element.7), channel_id=1, source_target_pairs={{1,2},{3,4},{5,6},{7,0},{2,1},{4,3},{6,5},{0,7},{9,10},{11,12},{13... | collective-permute-start | bytes 30728 | tf_op jit(solution)/shard_map/ppermute | solution.py:483
  1.3 2.9 %collective-permute-start.1 = (f32[20,128]{1,0:T(8,128)S(1)}, f32[20,128]{1,0:T(8,128)S(1)}, u32[]{:S(2)}, u32[]{:S(2)}) collective-permute-start(f32[20,128]{1,0:T(8,128)S(1)} %get-tuple-element.8), channel_id=1, source_target_pairs={{0,1},{2,3},{4,5},{6,7},{1,0},{3,2},{5,4},{7,6},{8,9},{10,11},{12,... | collective-permute-start | bytes 30728 | tf_op jit(solution)/shard_map/ppermute | solution.py:483

commit v7 on v5

--- a/solution.py
+++ b/solution.py
@@ -243,6 +243,10 @@
     return [[(1.0 - table[i][j]) if i == j else -table[i][j] for j in range(5)] for i in range(5)]
 
 
+def minus_identity(table):
+    return [[(table[i][j] - 1.0) if i == j else table[i][j] for j in range(5)] for i in range(5)]
+
+
 def dense(table):
     return [[e if hasattr(e, "shape") else jnp.full((8, 128), e, jnp.float32) for e in row] for row in table]
 
@@ -322,9 +326,10 @@
     cells[-1] = [half_before(e, True) for e in cells[3]]
     cells[4] = [half_after(e, True) for e in cells[0]]
     cells[5] = [half_after(e, True) for e in cells[1]]
-    from_before, from_after, along_x = {}, {}, {}
+    from_before, from_after, along_x, tables = {}, {}, {}, {}
     for t in range(-2, 5):
         table, velocity, pressure = jacobian_entries(cells[t])
+        tables[t] = [[None if e is None else SCALE * e for e in x] for x in table]
         from_before[t] = scaled_plus(table, SCALE, SHARE)
         from_after[t] = scaled_plus(table, -SCALE, SHARE)
         along_x[t] = flux_along(cells[t], velocity, pressure, 0)
@@ -344,12 +349,22 @@
     right[-1] = mapped(half_before, right[3])
 
     def eliminated(t):
-        matrix = identity_minus(
-            add_tables(
-                multiply(from_after[t + 1], from_before[t]),
-                multiply(from_before[t - 1], from_after[t]),
+        if t == 2:
+            outer, inner = tables[t + 1], tables[t - 1]
+            matrix = multiply(add_tables(outer, inner), tables[t])
+            for i in range(5):
+                for j in range(5):
+                    if outer[i][j] is not None:
+                        change = SHARE * (outer[i][j] - inner[i][j])
+                        matrix[i][j] = change if matrix[i][j] is None else matrix[i][j] + change
+                matrix[i][i] = matrix[i][i] + (1.0 - 2.0 * SHARE * SHARE)
+        else:
+            matrix = identity_minus(
+                add_tables(
+                    multiply(from_after[t + 1], from_before[t]),
+                    multiply(from_before[t - 1], from_after[t]),
+                )
             )
-        )
         before = dense(multiply(from_before[t - 1], from_before[t - 2]))
         after = dense(multiply(from_after[t + 1], from_after[t + 2]))
         value = add_tables(
@@ -407,9 +422,10 @@
         towards = lambda x, y: [[in_top(a, b) for a, b in zip(p, q)] for p, q in zip(x, y)]
         prior, following = earlier(packed), later(packed)
         crossed = mapped(swapped_halves, towards(following, prior))
-        matrix = identity_minus(both_halves(multiply(packed, crossed)))
+        matrix = minus_identity(both_halves(multiply(packed, crossed)))
         beside = towards(earlier(value), later(value))
-        value = add_tables(value, both_halves(multiply(packed, beside)))
+        moved = both_halves(multiply(packed, beside))
+        value = add_tables(moved, value) if stride == 1 else minus(moved, value)
         if stride < 16:
             packed = multiply(packed, towards(prior, following))
             solved = solve(matrix, side_by_side(packed, value))
@@ -418,6 +434,7 @@
             value = solve(matrix, value)
         stride *= 2
 
+    value = mapped(lambda e: -e, value)
     last_block = ((row & 3) == 3) & (lane >= 112)
     ahead = mapped(lambda e: jnp.where(last_block, 0.0, blocks_after(e, 1)), value)
     around = [[in_top(a[0], b[0])] for a, b in zip(value, ahead)]

time: 44.9 us -> 44.9 us (level)
  no operation moved by 1% of the time
where the time goes in v7:
time: 44.9 us; the launch traced here: 44.6 us
  blocking collectives  36.7 us (82%)
  Pallas kernels  4.12 us (9%)
  waiting for transfers between devices  1.85 us (4%)
  starting transfers between devices  1.02 us (2%)
  local copies, waits for them, and re-layouts  0.79 us (2%)
    all_to_all x1, blocking collectives, per_device(): lax.all_to_all(packed.reshape(32, 1, 1280), 'gx', split_axis=0, concat_ax...  23 us
    all_to_all x1, blocking collectives, per_device(): lax.all_to_all(solved.reshape(32, 1, 640), 'gx', split_axis=0, concat_axi...  13.7 us
    pallas_call x4, Pallas kernels, call(): pl.pallas_call(kernel, out_shape=jax.ShapeDtypeStruct((rows, 128), jnp.fl...  3.94 us
    ppermute x2, waiting for transfers between devices, per_device(): lax.ppermute(edges[start], 'gy', pairs + [(b, a) for a, b in pairs])  1.85 us
    ppermute x2, starting transfers between devices, per_device(): lax.ppermute(edges[start], 'gy', pairs + [(b, a) for a, b in pairs])  1.02 us
  transfers between devices with their start and end apart: 2, of which 1 were waited for; matrix products, arithmetic and copies ran while one was open for 0% of the time, Pallas kernels for 1%

profile of v7, /device:TPU:6, one launch (start us, length us, event | category | flops | bytes accessed | tf_op | source)
XLA Modules:
  0.0 44.6 jit_solution(14595575318709270501)
XLA Ops:
  0.0 0.8 %fusion = (f32[1,8,4,128]{3,2,1,0:T(4,128)S(1)}, f32[1,8,4,128]{3,2,1,0:T(4,128)S(1)}, f32[1,8,4,128]{3,2,1,0:T(4,128)S(1)}, f32[1,8,4,128]{3,2,1,0:T(4,128)S(1)}, f32[1,8,4,128]{3,2,1,0:T(4,128)S(1)}) fusion(f32[5,8,4,128]{3,2,1,0:T(4,128)} %param.1), kind=kLoop, calls=%fused_computation | loop fusion | bytes 163840 | tf_op jit(solution)/shard_map/slice | solution.py:487
  0.8 0.2 shard_map.18
  1.0 0.1 collective-permute-start
  1.1 0.9 %collective-permute-start.1 = (f32[20,128]{1,0:T(8,128)S(1)}, f32[20,128]{1,0:T(8,128)S(1)}, u32[]{:S(2)}, u32[]{:S(2)}) collective-permute-start(f32[20,128]{1,0:T(8,128)S(1)} %get-tuple-element.8), channel_id=1, source_target_pairs={{1,2},{3,4},{5,6},{7,0},{2,1},{4,3},{6,5},{0,7},{9,10},{11,12},{13... | collective-permute-start | bytes 30728 | tf_op jit(solution)/shard_map/ppermute | solution.py:500
  2.0 0.4 shard_map.17.packed_ref
  2.4 0.0 collective-permute-done.odd_ref
  2.4 1.9 %collective-permute-done.1.even_ref = f32[20,128]{1,0:T(8,128)S(1)} collective-permute-done((f32[20,128]{1,0:T(8,128)S(1)}, f32[20,128]{1,0:T(8,128)S(1)}, u32[]{:S(2)}, u32[]{:S(2)}) %collective-permute-start.1) | collective-permute-done | bytes 10272 | tf_op jit(solution)/shard_map/ppermute | solution.py:500
  4.3 0.1 shard_map.19
  4.4 23.0 %all_to_all.10 = f32[32,1,1280]{2,1,0:T(1,128)S(1)} all-to-all(f32[32,1,1280]{2,1,0:T(1,128)S(1)} %bitcast.10), channel_id=1, replica_groups=mesh['gx'=32,'gy'=8] {'gx'}, dimensions={0} | all-to-all | bytes 327680 | tf_op jit(solution)/shard_map/all_to_all | solution.py:504
  27.4 2.5 %shard_map.20 = f32[160,128]{1,0:T(8,128)S(1)} custom-call(f32[320,128]{1,0:T(8,128)S(1)} %bitcast.11), custom_call_target="tpu_custom_call" | custom-call | tf_op jit(solution)/shard_map/pallas_call | solution.py:476
  29.9 13.7 %all_to_all.11 = f32[32,1,640]{2,1,0:T(1,128)S(1)} all-to-all(f32[32,1,640]{2,1,0:T(1,128)S(1)} %bitcast.13), channel_id=1, replica_groups=mesh['gx'=32,'gy'=8] {'gx'}, dimensions={0} | all-to-all | bytes 163840 | tf_op jit(solution)/shard_map/all_to_all | solution.py:508
  43.7 0.9 %shard_map.21 = f32[160,128]{1,0:T(8,128)} custom-call(f32[160,128]{1,0:T(8,128)S(1)} %bitcast.12), custom_call_target="tpu_custom_call" | custom-call | tf_op jit(solution)/shard_map/pallas_call | solution.py:476
Async XLA Ops:
  1.0 1.4 %collective-permute-start = (f32[20,128]{1,0:T(8,128)S(1)}, f32[20,128]{1,0:T(8,128)S(1)}, u32[]{:S(2)}, u32[]{:S(2)}) collective-permute-start(f32[20,128]{1,0:T(8,128)S(1)} %get-tuple-element.7), channel_id=1, source_target_pairs={{0,1},{2,3},{4,5},{6,7},{1,0},{3,2},{5,4},{7,6},{8,9},{10,11},{12,... | collective-permute-start | bytes 30728 | tf_op jit(solution)/shard_map/ppermute | solution.py:500
  1.1 3.2 %collective-permute-start.1 = (f32[20,128]{1,0:T(8,128)S(1)}, f32[20,128]{1,0:T(8,128)S(1)}, u32[]{:S(2)}, u32[]{:S(2)}) collective-permute-start(f32[20,128]{1,0:T(8,128)S(1)} %get-tuple-element.8), channel_id=1, source_target_pairs={{1,2},{3,4},{5,6},{7,0},{2,1},{4,3},{6,5},{0,7},{9,10},{11,12},{13... | collective-permute-start | bytes 30728 | tf_op jit(solution)/shard_map/ppermute | solution.py:500

commit v8 on v7

--- a/solution.py
+++ b/solution.py
@@ -416,7 +416,7 @@
     packed, value = columns_of(solved, 0, 5), columns_of(solved, 5, 6)
 
     stride = 1
-    while stride < 32:
+    while stride < 16:
         earlier = lambda table: mapped(lambda e: blocks_before(e, stride), table)
         later = lambda table: mapped(lambda e: blocks_after(e, stride), table)
         towards = lambda x, y: [[in_top(a, b) for a, b in zip(p, q)] for p, q in zip(x, y)]
@@ -426,14 +426,16 @@
         beside = towards(earlier(value), later(value))
         moved = both_halves(multiply(packed, beside))
         value = add_tables(moved, value) if stride == 1 else minus(moved, value)
-        if stride < 16:
-            packed = multiply(packed, towards(prior, following))
-            solved = solve(matrix, side_by_side(packed, value))
-            packed, value = columns_of(solved, 0, 5), columns_of(solved, 5, 6)
-        else:
-            value = solve(matrix, value)
+        packed = multiply(packed, towards(prior, following))
+        solved = solve(matrix, side_by_side(packed, value))
+        packed, value = columns_of(solved, 0, 5), columns_of(solved, 5, 6)
         stride *= 2
 
+    other_half = (row < 4) == ((row & 3) < 2)
+    only = mapped(lambda e: jnp.where(other_half, swapped_halves(e), e), packed)
+    partner = lambda table: mapped(lambda e: roll_rows(e, 2), table)
+    matrix = minus_identity(multiply(only, partner(only)))
+    value = solve(matrix, minus(multiply(only, partner(value)), value))
     value = mapped(lambda e: -e, value)
     last_block = ((row & 3) == 3) & (lane >= 112)
     ahead = mapped(lambda e: jnp.where(last_block, 0.0, blocks_after(e, 1)), value)

time: 44.9 us -> 44.9 us (level)
  no operation moved by 1% of the time
where the time goes in v8:
time: 44.9 us; the launch traced here: 44.5 us
  blocking collectives  36.7 us (82%)
  Pallas kernels  4.1 us (9%)
  waiting for transfers between devices  1.85 us (4%)
  starting transfers between devices  1.02 us (2%)
  local copies, waits for them, and re-layouts  0.79 us (2%)
    all_to_all x1, blocking collectives, per_device(): lax.all_to_all(packed.reshape(32, 1, 1280), 'gx', split_axis=0, concat_ax...  23 us
    all_to_all x1, blocking collectives, per_device(): lax.all_to_all(solved.reshape(32, 1, 640), 'gx', split_axis=0, concat_axi...  13.7 us
    pallas_call x4, Pallas kernels, call(): pl.pallas_call(kernel, out_shape=jax.ShapeDtypeStruct((rows, 128), jnp.fl...  3.92 us
    ppermute x2, waiting for transfers between devices, per_device(): lax.ppermute(edges[start], 'gy', pairs + [(b, a) for a, b in pairs])  1.85 us
    ppermute x2, starting transfers between devices, per_device(): lax.ppermute(edges[start], 'gy', pairs + [(b, a) for a, b in pairs])  1.02 us
  transfers between devices with their start and end apart: 2, of which 1 were waited for; matrix products, arithmetic and copies ran while one was open for 0% of the time, Pallas kernels for 1%

profile of v8, /device:TPU:6, one launch (start us, length us, event | category | flops | bytes accessed | tf_op | source)
XLA Modules:
  0.0 44.5 jit_solution(7735641645652036861)
XLA Ops:
  0.0 0.8 %fusion = (f32[1,8,4,128]{3,2,1,0:T(4,128)S(1)}, f32[1,8,4,128]{3,2,1,0:T(4,128)S(1)}, f32[1,8,4,128]{3,2,1,0:T(4,128)S(1)}, f32[1,8,4,128]{3,2,1,0:T(4,128)S(1)}, f32[1,8,4,128]{3,2,1,0:T(4,128)S(1)}) fusion(f32[5,8,4,128]{3,2,1,0:T(4,128)} %param.1), kind=kLoop, calls=%fused_computation | loop fusion | bytes 163840 | tf_op jit(solution)/shard_map/slice | solution.py:489
  0.8 0.2 shard_map.18
  1.0 0.1 collective-permute-start
  1.1 0.9 %collective-permute-start.1 = (f32[20,128]{1,0:T(8,128)S(1)}, f32[20,128]{1,0:T(8,128)S(1)}, u32[]{:S(2)}, u32[]{:S(2)}) collective-permute-start(f32[20,128]{1,0:T(8,128)S(1)} %get-tuple-element.8), channel_id=1, source_target_pairs={{1,2},{3,4},{5,6},{7,0},{2,1},{4,3},{6,5},{0,7},{9,10},{11,12},{13... | collective-permute-start | bytes 30728 | tf_op jit(solution)/shard_map/ppermute | solution.py:502
  2.0 0.4 shard_map.17.packed_ref
  2.4 0.0 collective-permute-done.odd_ref
  2.4 1.9 %collective-permute-done.1.even_ref = f32[20,128]{1,0:T(8,128)S(1)} collective-permute-done((f32[20,128]{1,0:T(8,128)S(1)}, f32[20,128]{1,0:T(8,128)S(1)}, u32[]{:S(2)}, u32[]{:S(2)}) %collective-permute-start.1) | collective-permute-done | bytes 10272 | tf_op jit(solution)/shard_map/ppermute | solution.py:502
  4.3 0.1 shard_map.19
  4.4 23.0 %all_to_all.10 = f32[32,1,1280]{2,1,0:T(1,128)S(1)} all-to-all(f32[32,1,1280]{2,1,0:T(1,128)S(1)} %bitcast.10), channel_id=1, replica_groups=mesh['gx'=32,'gy'=8] {'gx'}, dimensions={0} | all-to-all | bytes 327680 | tf_op jit(solution)/shard_map/all_to_all | solution.py:506
  27.4 2.5 %shard_map.20 = f32[160,128]{1,0:T(8,128)S(1)} custom-call(f32[320,128]{1,0:T(8,128)S(1)} %bitcast.11), custom_call_target="tpu_custom_call" | custom-call | tf_op jit(solution)/shard_map/pallas_call | solution.py:478
  29.9 13.7 %all_to_all.11 = f32[32,1,640]{2,1,0:T(1,128)S(1)} all-to-all(f32[32,1,640]{2,1,0:T(1,128)S(1)} %bitcast.13), channel_id=1, replica_groups=mesh['gx'=32,'gy'=8] {'gx'}, dimensions={0} | all-to-all | bytes 163840 | tf_op jit(solution)/shard_map/all_to_all | solution.py:510
  43.7 0.9 %shard_map.21 = f32[160,128]{1,0:T(8,128)} custom-call(f32[160,128]{1,0:T(8,128)S(1)} %bitcast.12), custom_call_target="tpu_custom_call" | custom-call | tf_op jit(solution)/shard_map/pallas_call | solution.py:478
Async XLA Ops:
  1.0 1.4 %collective-permute-start = (f32[20,128]{1,0:T(8,128)S(1)}, f32[20,128]{1,0:T(8,128)S(1)}, u32[]{:S(2)}, u32[]{:S(2)}) collective-permute-start(f32[20,128]{1,0:T(8,128)S(1)} %get-tuple-element.7), channel_id=1, source_target_pairs={{0,1},{2,3},{4,5},{6,7},{1,0},{3,2},{5,4},{7,6},{8,9},{10,11},{12,... | collective-permute-start | bytes 30728 | tf_op jit(solution)/shard_map/ppermute | solution.py:502
  1.1 3.2 %collective-permute-start.1 = (f32[20,128]{1,0:T(8,128)S(1)}, f32[20,128]{1,0:T(8,128)S(1)}, u32[]{:S(2)}, u32[]{:S(2)}) collective-permute-start(f32[20,128]{1,0:T(8,128)S(1)} %get-tuple-element.8), channel_id=1, source_target_pairs={{1,2},{3,4},{5,6},{7,0},{2,1},{4,3},{6,5},{0,7},{9,10},{11,12},{13... | collective-permute-start | bytes 30728 | tf_op jit(solution)/shard_map/ppermute | solution.py:502
